TPU v7x, 32 devices: a whole 2x2x4 slice. The times are simulated.
32 devices in a mesh: dp: 8 (over z, core), mp: 4 (over y, x).
Axes of the slice: x: 2, y: 2, z: 4, core: 2. Of those that a mesh axis runs over, the one named last changes fastest.
Arguments:
- latents: bfloat16 [8192, 1024], P(('dp', 'mp')), may hold values from -6 to 6
- pixels: bfloat16 [16, 16384, 261], P('dp', 'mp'), may hold values from -6 to 6
- pixel_counts: int32 [16], P('dp'), may hold values from 1 to 16384, as said below
- cross_query: bfloat16 [1024, 1024], P(None, ('dp', 'mp')), may hold values from -0.1875 to 0.1875
- cross_key: bfloat16 [261, 1024], P(None, ('dp', 'mp')), may hold values from -0.375 to 0.375
- cross_value: bfloat16 [261, 1024], P(None, ('dp', 'mp')), may hold values from -0.375 to 0.375
- cross_out: bfloat16 [1024, 1024], P(None, ('dp', 'mp')), may hold values from -6 to 6
- cross_up: bfloat16 [1024, 1024], P(None, ('dp', 'mp')), may hold values from -0.1875 to 0.1875
- cross_down: bfloat16 [1024, 1024], P(None, ('dp', 'mp')), may hold values from -0.1875 to 0.1875
- block_qkv: bfloat16 [2, 1024, 3, 1024], P(None, 'dp', None, 'mp'), may hold values from -0.1875 to 0.1875
- block_out: bfloat16 [2, 1024, 1024], P(None, 'dp', 'mp'), may hold values from -3 to 3
- block_up: bfloat16 [2, 1024, 1024], P(None, 'dp', 'mp'), may hold values from -0.1875 to 0.1875
- block_down: bfloat16 [2, 1024, 1024], P(None, 'dp', 'mp'), may hold values from -0.1875 to 0.1875
- norm_gains: bfloat16 [6, 1024], P(None, ('dp', 'mp')), may hold values from 0.5 to 1.5
- norm_biases: bfloat16 [6, 1024], P(None, ('dp', 'mp')), may hold values from -1 to 1
- pixel_gain: bfloat16 [261], replicated, may hold values from 0.5 to 1.5
- pixel_bias: bfloat16 [261], replicated, may hold values from -1 to 1
- cotangent: bfloat16 [8192, 1024], P(('dp', 'mp')), may hold values from -6 to 6
Outputs:
- latents_out: bfloat16 [8192, 1024], P(('dp', 'mp'))
- latent_grad: bfloat16 [8192, 1024], P(('dp', 'mp'))
- pixel_grad: bfloat16 [16, 16384, 261], P('dp', 'mp')
- cross_query_grad: float32 [1024, 1024], P(None, ('dp', 'mp'))
- cross_key_grad: float32 [261, 1024], P(None, ('dp', 'mp'))
- cross_value_grad: float32 [261, 1024], P(None, ('dp', 'mp'))
- cross_out_grad: float32 [1024, 1024], P(None, ('dp', 'mp'))
- cross_up_grad: float32 [1024, 1024], P(None, ('dp', 'mp'))
- cross_down_grad: float32 [1024, 1024], P(None, ('dp', 'mp'))
- block_qkv_grad: float32 [2, 1024, 3, 1024], P(None, 'dp', None, 'mp')
- block_out_grad: float32 [2, 1024, 1024], P(None, 'dp', 'mp')
- block_up_grad: float32 [2, 1024, 1024], P(None, 'dp', 'mp')
- block_down_grad: float32 [2, 1024, 1024], P(None, 'dp', 'mp')
- norm_gain_grad: float32 [6, 1024], P(None, ('dp', 'mp'))
- norm_bias_grad: float32 [6, 1024], P(None, ('dp', 'mp'))
- pixel_gain_grad: float32 [261], replicated
- pixel_bias_grad: float32 [261], replicated
Inputs may be any that keep to these rules, and one draw needn't show every extreme that they name: In each aligned group of 2 items one item, drawn from the seed, has exactly 16384 pixels; item i's pixels fill slots 0 to pixel_counts[i] - 1, the remaining slots are padding.
All inputs are finite; a program needn't handle non-finite values.
Results may differ from a plain program's by a relative error of at most 0.02.
Values may be sent and summed in bfloat16 or wider, within the bound.
A program may use at most 320 MiB of HBM per device.

v0:
```python
import math

import jax
import jax.numpy as jnp
from jax import lax
from jax.sharding import PartitionSpec as P

HD = 128


norm_eps = 1e-05
masked_score = -1e30


def joined(value, axis, join):
    pieces = jax.tree.map(lambda part: lax.all_gather(part, axis), value)
    head = jax.tree.map(lambda part: part[0], pieces)
    tail = jax.tree.map(lambda part: part[1:], pieces)
    running, _ = lax.scan(lambda running, share: (join(running, share), None), head, tail)
    return running


def layer_norm(features, gain_row, offset):
    average = jnp.mean(features, axis=-1, keepdims=True)
    centered = features - average
    variance = jnp.mean(centered * centered, axis=-1, keepdims=True)
    return centered * lax.rsqrt(variance + norm_eps) * gain_row + offset


def norm_back(features, gain_row, offset, upstream):
    _, pullback = jax.vjp(layer_norm, features, gain_row, offset)
    return pullback(upstream)


def gelu_back(hidden, upstream):
    _, pullback = jax.vjp(jax.nn.gelu, hidden)
    return pullback(upstream)[0]


def matmul(left_side, right_side):
    return jnp.dot(left_side, right_side, preferred_element_type=jnp.float32)


def times_transposed(left_side, right_side):
    return lax.dot_general(
        left_side, right_side, (((1,), (1,)), ((), ())), preferred_element_type=jnp.float32
    )


def transposed_times(left_side, right_side):
    return lax.dot_general(
        left_side, right_side, (((0,), (0,)), ((), ())), preferred_element_type=jnp.float32
    )


def gather_rows(payload):
    return lax.all_gather(payload, "mp", axis=0, tiled=True)


def gather_grads(payload):
    return lax.all_gather(payload, "mp", axis=0, tiled=True)


def sum_branch(row_term, own_rows):
    return lax.psum_scatter(
        row_term(jnp.int32(0), own_rows * lax.axis_size("mp")).astype(jnp.bfloat16),
        "mp",
        scatter_dimension=0,
        tiled=True,
    ).astype(jnp.float32)


def sum_inputs(row_term, own_rows):
    return lax.psum_scatter(
        row_term(jnp.int32(0), own_rows * lax.axis_size("mp")).astype(jnp.bfloat16),
        "mp",
        scatter_dimension=0,
        tiled=True,
    ).astype(jnp.float32)


def slicer(source):

    def row_term(first_row, row_count):
        return source

    return row_term


def product_term(source, weight, formula):

    def row_term(first_row, row_count):
        return jnp.einsum(formula, source, weight, preferred_element_type=jnp.float32)

    return row_term


def merge_stats(earlier, latter):
    row_top = jnp.maximum(earlier[0], latter[0])
    return (
        row_top,
        earlier[1] * jnp.exp(earlier[0] - row_top) + latter[1] * jnp.exp(latter[0] - row_top),
    )


def cross_params(
    cross_query, cross_key, cross_value, cross_out, cross_up, cross_down, norm_gains, norm_biases
):
    return (
        lax.all_gather(cross_query, ("dp", "mp"), axis=1, tiled=True),
        lax.all_gather(cross_key, ("dp", "mp"), axis=1, tiled=True),
        lax.all_gather(cross_value, ("dp", "mp"), axis=1, tiled=True),
        lax.all_gather(cross_out, ("dp", "mp"), axis=1, tiled=True),
        lax.all_gather(cross_up, ("dp", "mp"), axis=1, tiled=True),
        lax.all_gather(cross_down, ("dp", "mp"), axis=1, tiled=True),
        lax.all_gather(norm_gains, ("dp", "mp"), axis=1, tiled=True),
        lax.all_gather(norm_biases, ("dp", "mp"), axis=1, tiled=True),
    )


def block_weights(block_qkv, block_out, block_up, block_down, layer_index):
    return (
        lax.all_gather(block_qkv[layer_index], "dp", axis=0, tiled=True),
        lax.all_gather(block_out[layer_index], "dp", axis=0, tiled=True),
        lax.all_gather(block_up[layer_index], "dp", axis=0, tiled=True),
        lax.all_gather(block_down[layer_index], "dp", axis=0, tiled=True),
    )


def block_forward(current, layer_index, gain_rows, bias_rows, block_params, item_count):
    qkv_weight, out_weight, up_weight, down_weight = block_weights(
        block_params[0], block_params[1], block_params[2], block_params[3], layer_index
    )
    own_rows = current.shape[0]
    group_rows = own_rows * lax.axis_size("mp")
    latents_item = group_rows // item_count
    head_cols = qkv_weight.shape[2]
    heads_local = head_cols // HD
    block_scale = 1.0 / math.sqrt(HD)
    normed = layer_norm(
        current, gain_rows[2 + 2 * layer_index], bias_rows[2 + 2 * layer_index]
    ).astype(jnp.bfloat16)
    normed_group = gather_rows(normed)
    projected = jnp.einsum(
        "rd,dtk->rtk", normed_group, qkv_weight, preferred_element_type=jnp.float32
    ).astype(jnp.bfloat16)
    heads_view = projected.reshape(item_count, latents_item, 3, heads_local, HD)
    raw_scores = (
        jnp.einsum(
            "iqhe,ikhe->ihqk",
            heads_view[:, :, 0],
            heads_view[:, :, 1],
            preferred_element_type=jnp.float32,
        )
        * block_scale
    )
    row_top = jnp.max(raw_scores, axis=-1, keepdims=True)
    lifted = jnp.exp(raw_scores - row_top)
    row_total = jnp.sum(lifted, axis=-1, keepdims=True)
    attention = lifted / row_total
    log_total = row_top + jnp.log(row_total)
    context = jnp.einsum(
        "ihqk,ikhe->iqhe",
        attention.astype(jnp.bfloat16),
        heads_view[:, :, 2],
        preferred_element_type=jnp.float32,
    )
    context = context.astype(jnp.bfloat16).reshape(group_rows, head_cols)
    middle = current + sum_branch(product_term(context, out_weight, "rk,dk->rd"), own_rows)
    hidden_in = layer_norm(
        middle, gain_rows[3 + 2 * layer_index], bias_rows[3 + 2 * layer_index]
    ).astype(jnp.bfloat16)
    hidden_group = gather_rows(hidden_in)
    hidden = matmul(hidden_group, up_weight)
    active = jax.nn.gelu(hidden).astype(jnp.bfloat16)
    result = middle + sum_branch(product_term(active, down_weight, "rf,df->rd"), own_rows)
    stored = (
        qkv_weight,
        out_weight,
        up_weight,
        down_weight,
        normed_group,
        projected,
        log_total,
        context,
        middle,
        hidden_group,
        hidden,
        active,
    )
    return (result, stored)


def block_backward(upstream, current, layer_index, gain_rows, bias_rows, stored, item_count):
    (
        qkv_weight,
        out_weight,
        up_weight,
        down_weight,
        normed_group,
        projected,
        log_total,
        context,
        middle,
        hidden_group,
        hidden,
        active,
    ) = stored
    own_rows = upstream.shape[0]
    group_rows = own_rows * lax.axis_size("mp")
    latents_item = group_rows // item_count
    head_cols = qkv_weight.shape[2]
    heads_local = head_cols // HD
    block_scale = 1.0 / math.sqrt(HD)
    down_group = gather_grads(upstream.astype(jnp.bfloat16))
    down_grad = transposed_times(down_group, active)
    active_cot = matmul(down_group, down_weight)
    hidden_cot = gelu_back(hidden, active_cot).astype(jnp.bfloat16)
    up_grad = transposed_times(hidden_group, hidden_cot)
    hidden_in_cot = sum_inputs(product_term(hidden_cot, up_weight, "rf,df->rd"), own_rows)
    middle_cot, gain_late, bias_late = norm_back(
        middle, gain_rows[3 + 2 * layer_index], bias_rows[3 + 2 * layer_index], hidden_in_cot
    )
    middle_cot = middle_cot + upstream
    out_group = gather_grads(middle_cot.astype(jnp.bfloat16))
    out_grad = transposed_times(out_group, context)
    context_cot = (
        matmul(out_group, out_weight)
        .astype(jnp.bfloat16)
        .reshape(item_count, latents_item, heads_local, HD)
    )
    heads_view = projected.reshape(item_count, latents_item, 3, heads_local, HD)
    queries = heads_view[:, :, 0]
    key_rows = heads_view[:, :, 1]
    value_rows = heads_view[:, :, 2]
    raw_scores = (
        jnp.einsum("iqhe,ikhe->ihqk", queries, key_rows, preferred_element_type=jnp.float32)
        * block_scale
    )
    attention = jnp.exp(raw_scores - log_total)
    value_cot = jnp.einsum(
        "ihqk,iqhe->ikhe",
        attention.astype(jnp.bfloat16),
        context_cot,
        preferred_element_type=jnp.float32,
    )
    prob_cot = jnp.einsum(
        "iqhe,ikhe->ihqk", context_cot, value_rows, preferred_element_type=jnp.float32
    )
    row_terms = jnp.sum(attention * prob_cot, axis=-1, keepdims=True)
    score_cot = (attention * (prob_cot - row_terms) * block_scale).astype(jnp.bfloat16)
    query_cot = jnp.einsum(
        "ihqk,ikhe->iqhe", score_cot, key_rows, preferred_element_type=jnp.float32
    )
    key_cot = jnp.einsum("ihqk,iqhe->ikhe", score_cot, queries, preferred_element_type=jnp.float32)
    projected_cot = jnp.stack(
        [
            query_cot.astype(jnp.bfloat16),
            key_cot.astype(jnp.bfloat16),
            value_cot.astype(jnp.bfloat16),
        ],
        axis=2,
    )
    projected_cot = projected_cot.reshape(group_rows, 3, head_cols)
    qkv_grad = jnp.einsum(
        "rd,rtk->dtk", normed_group, projected_cot, preferred_element_type=jnp.float32
    )
    normed_cot = sum_inputs(product_term(projected_cot, qkv_weight, "rtk,dtk->rd"), own_rows)
    input_cot, gain_early, bias_early = norm_back(
        current, gain_rows[2 + 2 * layer_index], bias_rows[2 + 2 * layer_index], normed_cot
    )
    input_cot = input_cot + middle_cot
    summed = (
        lax.psum_scatter(
            qkv_grad.astype(jnp.bfloat16), "dp", scatter_dimension=0, tiled=True
        ).astype(jnp.float32),
        lax.psum_scatter(
            out_grad.astype(jnp.bfloat16), "dp", scatter_dimension=0, tiled=True
        ).astype(jnp.float32),
        lax.psum_scatter(
            up_grad.astype(jnp.bfloat16), "dp", scatter_dimension=0, tiled=True
        ).astype(jnp.float32),
        lax.psum_scatter(
            down_grad.astype(jnp.bfloat16), "dp", scatter_dimension=0, tiled=True
        ).astype(jnp.float32),
    )
    return (input_cot, summed, (gain_early, bias_early, gain_late, bias_late))


def shards(
    latents,
    pixels,
    pixel_counts,
    cross_query,
    cross_key,
    cross_value,
    cross_out,
    cross_up,
    cross_down,
    block_qkv,
    block_out,
    block_up,
    block_down,
    norm_gains,
    norm_biases,
    pixel_gain,
    pixel_bias,
    cotangent,
):
    layers = block_qkv.shape[0]
    item_count = pixels.shape[0]
    pixel_rows = pixels.shape[1]
    own_rows = latents.shape[0]
    model_width = latents.shape[1]
    group_rows = own_rows * lax.axis_size("mp")
    latents_item = group_rows // item_count
    cross_scale = 1.0 / math.sqrt(model_width)
    block_params = (block_qkv, block_out, block_up, block_down)
    forward_params = cross_params(
        cross_query,
        cross_key,
        cross_value,
        cross_out,
        cross_up,
        cross_down,
        norm_gains,
        norm_biases,
    )
    (
        query_weight,
        key_weight,
        value_weight,
        out_weight,
        up_weight,
        down_weight,
        gain_table,
        bias_table,
    ) = forward_params
    gain_rows = gain_table.astype(jnp.float32)
    bias_rows = bias_table.astype(jnp.float32)
    start_rows = latents.astype(jnp.float32)
    query_in = layer_norm(start_rows, gain_rows[0], bias_rows[0]).astype(jnp.bfloat16)
    query_own = matmul(query_in, query_weight).astype(jnp.bfloat16)
    query_group = gather_rows(query_own).reshape(item_count, latents_item, model_width)
    pixel_floats = pixels.astype(jnp.float32)
    pixel_gain_row = pixel_gain.astype(jnp.float32)
    pixel_bias_row = pixel_bias.astype(jnp.float32)
    pixel_in = layer_norm(pixel_floats, pixel_gain_row, pixel_bias_row).astype(jnp.bfloat16)
    pair_weight = jnp.concatenate([key_weight, value_weight], axis=1)
    pair_rows = jnp.einsum(
        "ipc,cd->ipd", pixel_in, pair_weight, preferred_element_type=jnp.float32
    ).astype(jnp.bfloat16)
    key_rows = pair_rows[:, :, :model_width]
    value_rows = pair_rows[:, :, model_width:]
    positions = lax.axis_index("mp") * pixel_rows + jnp.arange(pixel_rows, dtype=jnp.int32)
    present = positions[None, :] < pixel_counts[:, None]
    present_mask = present.astype(jnp.float32)[:, None, :]

    def cross_scores():
        raw_scores = (
            jnp.einsum("iqd,ipd->iqp", query_group, key_rows, preferred_element_type=jnp.float32)
            * cross_scale
        )
        return jnp.where(present[:, None, :], raw_scores, masked_score)

    scores = cross_scores()
    local_top = jnp.max(scores, axis=-1)
    local_total = jnp.sum(jnp.exp(scores - local_top[:, :, None]) * present_mask, axis=-1)
    group_top, group_total = joined((local_top, local_total), "mp", merge_stats)
    log_total = (group_top + jnp.log(group_total))[:, :, None]
    attention = jnp.exp(scores - log_total) * present_mask
    attended = jnp.einsum(
        "iqp,ipd->iqd",
        attention.astype(jnp.bfloat16),
        value_rows,
        preferred_element_type=jnp.float32,
    )
    attended = attended.reshape(group_rows, model_width)
    context_own = sum_branch(slicer(attended), own_rows).astype(jnp.bfloat16)
    after_cross = start_rows + matmul(context_own, out_weight)
    cross_hidden_in = layer_norm(after_cross, gain_rows[1], bias_rows[1]).astype(jnp.bfloat16)
    cross_hidden = matmul(cross_hidden_in, up_weight)
    cross_active = jax.nn.gelu(cross_hidden).astype(jnp.bfloat16)
    current = after_cross + matmul(cross_active, down_weight)
    inputs_kept = []
    stored_all = []
    for layer_index in range(layers):
        inputs_kept.append(current)
        current, stored = block_forward(
            current, layer_index, gain_rows, bias_rows, block_params, item_count
        )
        stored_all.append(stored)
    latents_out = current.astype(jnp.bfloat16)
    later_params = cross_params(
        cross_query,
        cross_key,
        cross_value,
        cross_out,
        cross_up,
        cross_down,
        norm_gains,
        norm_biases,
    )
    (
        query_weight,
        key_weight,
        value_weight,
        out_weight,
        up_weight,
        down_weight,
        gain_table,
        bias_table,
    ) = later_params
    gain_rows = gain_table.astype(jnp.float32)
    bias_rows = bias_table.astype(jnp.float32)
    gain_parts = [None] * (2 * layers + 2)
    bias_parts = [None] * (2 * layers + 2)
    qkv_grads = [None] * layers
    out_grads = [None] * layers
    up_grads = [None] * layers
    down_grads = [None] * layers
    current_cot = cotangent.astype(jnp.float32)
    for layer_index in reversed(range(layers)):
        _, stored = block_forward(
            inputs_kept[layer_index], layer_index, gain_rows, bias_rows, block_params, item_count
        )
        current_cot, summed, norm_parts = block_backward(
            current_cot,
            inputs_kept[layer_index],
            layer_index,
            gain_rows,
            bias_rows,
            stored,
            item_count,
        )
        qkv_grads[layer_index] = summed[0]
        out_grads[layer_index] = summed[1]
        up_grads[layer_index] = summed[2]
        down_grads[layer_index] = summed[3]
        gain_parts[2 + 2 * layer_index] = norm_parts[0]
        bias_parts[2 + 2 * layer_index] = norm_parts[1]
        gain_parts[3 + 2 * layer_index] = norm_parts[2]
        bias_parts[3 + 2 * layer_index] = norm_parts[3]
    down_in = current_cot.astype(jnp.bfloat16)
    cross_down_grad = transposed_times(cross_active, down_in)
    active_cot = times_transposed(down_in, down_weight)
    hidden_cot = gelu_back(cross_hidden, active_cot).astype(jnp.bfloat16)
    cross_up_grad = transposed_times(cross_hidden_in, hidden_cot)
    hidden_in_cot = times_transposed(hidden_cot, up_weight)
    after_cot, gain_parts[1], bias_parts[1] = norm_back(
        after_cross, gain_rows[1], bias_rows[1], hidden_in_cot
    )
    after_cot = after_cot + current_cot
    out_in = after_cot.astype(jnp.bfloat16)
    cross_out_grad = transposed_times(context_own, out_in)
    context_cot = times_transposed(out_in, out_weight).astype(jnp.bfloat16)
    context_group = gather_grads(context_cot).reshape(item_count, latents_item, model_width)
    scores = cross_scores()
    attention = jnp.exp(scores - log_total) * present_mask
    value_cot = jnp.einsum(
        "iqp,iqd->ipd",
        attention.astype(jnp.bfloat16),
        context_group,
        preferred_element_type=jnp.float32,
    ).astype(jnp.bfloat16)
    prob_cot = jnp.einsum(
        "iqd,ipd->iqp", context_group, value_rows, preferred_element_type=jnp.float32
    )
    row_part = jnp.sum(attention * prob_cot, axis=-1)
    row_terms = lax.psum(row_part, "mp")
    score_cot = (attention * (prob_cot - row_terms[:, :, None]) * cross_scale).astype(jnp.bfloat16)
    query_part = jnp.einsum(
        "iqp,ipd->iqd", score_cot, key_rows, preferred_element_type=jnp.float32
    ).reshape(group_rows, model_width)
    query_cot = sum_inputs(slicer(query_part), own_rows).astype(jnp.bfloat16)
    key_cot = jnp.einsum(
        "iqp,iqd->ipd", score_cot, query_group, preferred_element_type=jnp.float32
    ).astype(jnp.bfloat16)
    cross_query_grad = transposed_times(query_in, query_cot)
    query_in_cot = times_transposed(query_cot, query_weight)
    start_cot, gain_parts[0], bias_parts[0] = norm_back(
        start_rows, gain_rows[0], bias_rows[0], query_in_cot
    )
    latent_grad = (start_cot + after_cot).astype(jnp.bfloat16)
    pair_weight = jnp.concatenate([key_weight, value_weight], axis=1)
    pair_cot = jnp.concatenate([key_cot, value_cot], axis=2)
    pair_grad = jnp.einsum("ipc,ipd->cd", pixel_in, pair_cot, preferred_element_type=jnp.float32)
    cross_key_grad = pair_grad[:, :model_width]
    cross_value_grad = pair_grad[:, model_width:]
    pixel_in_cot = jnp.einsum(
        "ipd,cd->ipc", pair_cot, pair_weight, preferred_element_type=jnp.float32
    )
    pixel_cot, pixel_gain_part, pixel_bias_part = norm_back(
        pixel_floats, pixel_gain_row, pixel_bias_row, pixel_in_cot
    )
    pixel_grad = pixel_cot.astype(jnp.bfloat16)
    gain_stack = jnp.stack(gain_parts, axis=0)
    bias_stack = jnp.stack(bias_parts, axis=0)
    cross_summed = (
        lax.psum_scatter(cross_query_grad, ("dp", "mp"), scatter_dimension=1, tiled=True),
        lax.psum_scatter(cross_key_grad, ("dp", "mp"), scatter_dimension=1, tiled=True),
        lax.psum_scatter(cross_value_grad, ("dp", "mp"), scatter_dimension=1, tiled=True),
        lax.psum_scatter(cross_out_grad, ("dp", "mp"), scatter_dimension=1, tiled=True),
        lax.psum_scatter(cross_up_grad, ("dp", "mp"), scatter_dimension=1, tiled=True),
        lax.psum_scatter(cross_down_grad, ("dp", "mp"), scatter_dimension=1, tiled=True),
        lax.psum_scatter(gain_stack, ("dp", "mp"), scatter_dimension=1, tiled=True),
        lax.psum_scatter(bias_stack, ("dp", "mp"), scatter_dimension=1, tiled=True),
    )
    pixel_gain_grad, pixel_bias_grad = lax.psum((pixel_gain_part, pixel_bias_part), ("dp", "mp"))
    return (
        latents_out,
        latent_grad,
        pixel_grad,
        cross_summed[0],
        cross_summed[1],
        cross_summed[2],
        cross_summed[3],
        cross_summed[4],
        cross_summed[5],
        jnp.stack(qkv_grads, axis=0),
        jnp.stack(out_grads, axis=0),
        jnp.stack(up_grads, axis=0),
        jnp.stack(down_grads, axis=0),
        cross_summed[6],
        cross_summed[7],
        pixel_gain_grad,
        pixel_bias_grad,
    )


def solution(mesh):
    return jax.shard_map(
        shards,
        mesh=mesh,
        in_specs=(
            P(("dp", "mp"), None),
            P("dp", "mp", None),
            P("dp"),
            P(None, ("dp", "mp")),
            P(None, ("dp", "mp")),
            P(None, ("dp", "mp")),
            P(None, ("dp", "mp")),
            P(None, ("dp", "mp")),
            P(None, ("dp", "mp")),
            P(None, "dp", None, "mp"),
            P(None, "dp", "mp"),
            P(None, "dp", "mp"),
            P(None, "dp", "mp"),
            P(None, ("dp", "mp")),
            P(None, ("dp", "mp")),
            P(),
            P(),
            P(("dp", "mp"), None),
        ),
        out_specs=(
            P(("dp", "mp"), None),
            P(("dp", "mp"), None),
            P("dp", "mp", None),
            P(None, ("dp", "mp")),
            P(None, ("dp", "mp")),
            P(None, ("dp", "mp")),
            P(None, ("dp", "mp")),
            P(None, ("dp", "mp")),
            P(None, ("dp", "mp")),
            P(None, "dp", None, "mp"),
            P(None, "dp", "mp"),
            P(None, "dp", "mp"),
            P(None, "dp", "mp"),
            P(None, ("dp", "mp")),
            P(None, ("dp", "mp")),
            P(),
            P(),
        ),
        check_vma=False,
    )
```

profile of v0, /device:TPU:0, one launch (start us, length us, event | category | flops | bytes accessed | tf_op | source)
XLA Modules:
  0.0 2834.5 jit_solution(2472496699146115160)
XLA Ops:
  8.0 70.5 %all-gather.10 = bf16[32,32,6]{1,2,0:T(8,128)(2,1)S(1)} all-gather(bf16[1,32,6]{1,2,0:T(8,128)(2,1)} %bitcast.335), channel_id=1, replica_groups=mesh['dp'=8,'mp'=4] {'dp','mp'}, dimensions={0}, use_global_device_ids=true | all-gather | bytes 12672 | tf_op jit(solution)/shard_map/all_gather | solution.py:116
  78.6 63.9 %all-gather.11 = bf16[32,32,6]{1,2,0:T(8,128)(2,1)S(1)} all-gather(bf16[1,32,6]{1,2,0:T(8,128)(2,1)} %bitcast.336), channel_id=1, replica_groups=mesh['dp'=8,'mp'=4] {'dp','mp'}, dimensions={0}, use_global_device_ids=true | all-gather | bytes 12672 | tf_op jit(solution)/shard_map/all_gather | solution.py:117
  161.7 70.6 %all_gather.114 = bf16[261,1024]{0,1:T(8,128)(2,1)S(1)} all-gather(bf16[261,32]{0,1:T(8,128)(2,1)S(1)} %copy-done.77), channel_id=1, replica_groups=mesh['dp'=8,'mp'=4] {'dp','mp'}, dimensions={1}, use_global_device_ids=true | all-gather | bytes 551232 | tf_op jit(solution)/shard_map/all_gather | solution.py:111
  232.5 68.0 %all_gather.115 = bf16[261,1024]{0,1:T(8,128)(2,1)S(1)} all-gather(bf16[261,32]{0,1:T(8,128)(2,1)S(1)} %copy-done.78), channel_id=1, replica_groups=mesh['dp'=8,'mp'=4] {'dp','mp'}, dimensions={1}, use_global_device_ids=true | all-gather | bytes 551232 | tf_op jit(solution)/shard_map/all_gather | solution.py:112
  300.9 57.5 %convolution_convert_fusion = bf16[2,4096,2048]{2,1,0:T(8,128)(2,1)} fusion(bf16[261,1024]{1,0:T(8,128)(2,1)S(1)} %copy.170, bf16[261,1024]{1,0:T(8,128)(2,1)S(1)} %copy.169, f32[261]{0:T(512)S(1)} %convert_element_type.316, f32[261]{0:T(512)S(1)} %convert_element_type.315, f32[2,4096]{1,0:T(2,128)S(1)} %fusion.243, ...), kind=kOutput, calls=%fused_computation.10 | convolution fusion | flops 8789450752 | bytes 38967336 | tf_op jit(solution)/shard_map/ipc,cd->ipd/dot_general | solution.py:350
  451.4 56.6 %all-gather.37.cloned.1.call-done = bf16[1024,1024]{0,1:T(8,128)(2,1)} async-done(((bf16[1024,32]{0,1:T(8,128)(2,1)}), bf16[1024,1024]{0,1:T(8,128)(2,1)}) %all-gather.37.cloned.1.call-update) | async-done | bytes 2097168 | tf_op jit(solution)/shard_map/all_gather | solution.py:114
  510.4 56.0 %all-gather.39.cloned.1.call-done = bf16[1024,1024]{0,1:T(8,128)(2,1)} async-done(((bf16[1024,32]{0,1:T(8,128)(2,1)}), bf16[1024,1024]{0,1:T(8,128)(2,1)}) %all-gather.39.cloned.1.call-update) | async-done | bytes 2097168 | tf_op jit(solution)/shard_map/all_gather | solution.py:115
  595.2 36.6 %all-gather.41.cloned.1.call-done = bf16[1024,1024]{1,0:T(8,128)(2,1)} async-done(((bf16[256,1024]{1,0:T(8,128)(2,1)}), bf16[1024,1024]{1,0:T(8,128)(2,1)}) %all-gather.41.cloned.1.call-update) | async-done | bytes 2097168 | tf_op jit(solution)/shard_map/all_gather | solution.py:57
  653.2 35.3 %reduce-scatter.37.cloned.1.call-done = bf16[256,1024]{1,0:T(8,128)(2,1)} async-done(((bf16[1024,1024]{1,0:T(8,128)(2,1)}), bf16[256,1024]{1,0:T(8,128)(2,1)}) %reduce-scatter.37.cloned.1.call-update) | async-done | bytes 524304 | tf_op jit(solution)/shard_map/reduce_scatter | solution.py:65
  732.6 34.7 %reduce-scatter.39.cloned.1.call-done = bf16[256,1024]{1,0:T(8,128)(2,1)} async-done(((bf16[1024,1024]{1,0:T(8,128)(2,1)}), bf16[256,1024]{1,0:T(8,128)(2,1)}) %reduce-scatter.39.cloned.1.call-update) | async-done | bytes 524304 | tf_op jit(solution)/shard_map/reduce_scatter | solution.py:65
  796.4 36.7 %all-gather.45.cloned.1.call-done = bf16[1024,1024]{1,0:T(8,128)(2,1)} async-done(((bf16[256,1024]{1,0:T(8,128)(2,1)}), bf16[1024,1024]{1,0:T(8,128)(2,1)}) %all-gather.45.cloned.1.call-update) | async-done | bytes 2097168 | tf_op jit(solution)/shard_map/all_gather | solution.py:57
  858.2 35.3 %reduce-scatter.41.cloned.1.call-done = bf16[256,1024]{1,0:T(8,128)(2,1)} async-done(((bf16[1024,1024]{1,0:T(8,128)(2,1)}), bf16[256,1024]{1,0:T(8,128)(2,1)}) %reduce-scatter.41.cloned.1.call-update) | async-done | bytes 524304 | tf_op jit(solution)/shard_map/reduce_scatter | solution.py:65
  935.6 33.7 %all-gather.49.cloned.1.call-done = bf16[1024,1024]{1,0:T(8,128)(2,1)} async-done(((bf16[256,1024]{1,0:T(8,128)(2,1)}), bf16[1024,1024]{1,0:T(8,128)(2,1)}) %all-gather.49.cloned.1.call-update) | async-done | bytes 2097168 | tf_op jit(solution)/shard_map/all_gather | solution.py:61
  1013.1 35.9 %reduce-scatter.43.cloned.1.call-done = bf16[256,1024]{1,0:T(8,128)(2,1)} async-done(((bf16[1024,1024]{1,0:T(8,128)(2,1)}), bf16[256,1024]{1,0:T(8,128)(2,1)}) %reduce-scatter.43.cloned.1.call-update) | async-done | bytes 524304 | tf_op jit(solution)/shard_map/reduce_scatter | solution.py:65
  1055.0 35.2 %all-gather.51.cloned.1.call-done = bf16[1024,1024]{1,0:T(8,128)(2,1)} async-done(((bf16[256,1024]{1,0:T(8,128)(2,1)}), bf16[1024,1024]{1,0:T(8,128)(2,1)}) %all-gather.51.cloned.1.call-update) | async-done | bytes 2097168 | tf_op jit(solution)/shard_map/all_gather | solution.py:61
  1143.0 35.3 %reduce-scatter.47.cloned.1.call-done = bf16[256,1024]{1,0:T(8,128)(2,1)} async-done(((bf16[1024,1024]{1,0:T(8,128)(2,1)}), bf16[256,1024]{1,0:T(8,128)(2,1)}) %reduce-scatter.47.cloned.1.call-update) | async-done | bytes 524304 | tf_op jit(solution)/shard_map/reduce_scatter | solution.py:74
  1186.0 35.2 %all-gather.53.cloned.1.call-done = bf16[1024,1024]{1,0:T(8,128)(2,1)} async-done(((bf16[256,1024]{1,0:T(8,128)(2,1)}), bf16[1024,1024]{1,0:T(8,128)(2,1)}) %all-gather.53.cloned.1.call-update) | async-done | bytes 2097168 | tf_op jit(solution)/shard_map/all_gather | solution.py:61
  1226.5 35.3 %reduce-scatter.49.cloned.1.call-done = bf16[256,1024]{1,0:T(8,128)(2,1)} async-done(((bf16[1024,1024]{1,0:T(8,128)(2,1)}), bf16[256,1024]{1,0:T(8,128)(2,1)}) %reduce-scatter.49.cloned.1.call-update) | async-done | bytes 524304 | tf_op jit(solution)/shard_map/reduce_scatter | solution.py:74
  1267.6 35.4 %all-gather.55.cloned.1.call-done = bf16[1024,1024]{1,0:T(8,128)(2,1)} async-done(((bf16[256,1024]{1,0:T(8,128)(2,1)}), bf16[1024,1024]{1,0:T(8,128)(2,1)}) %all-gather.55.cloned.1.call-update) | async-done | bytes 2097168 | tf_op jit(solution)/shard_map/all_gather | solution.py:61
  1347.6 34.9 %reduce-scatter.51.cloned.1.call-done = bf16[256,1024]{1,0:T(8,128)(2,1)} async-done(((bf16[1024,1024]{1,0:T(8,128)(2,1)}), bf16[256,1024]{1,0:T(8,128)(2,1)}) %reduce-scatter.51.cloned.1.call-update) | async-done | bytes 524304 | tf_op jit(solution)/shard_map/reduce_scatter | solution.py:74
  1395.5 35.4 %all-gather.57.cloned.1.call-done = bf16[1024,1024]{1,0:T(8,128)(2,1)} async-done(((bf16[256,1024]{1,0:T(8,128)(2,1)}), bf16[1024,1024]{1,0:T(8,128)(2,1)}) %all-gather.57.cloned.1.call-update) | async-done | bytes 2097168 | tf_op jit(solution)/shard_map/all_gather | solution.py:61
  1722.2 33.0 %reduce-scatter.65.cloned.1.call-done = bf16[128,3,256]{2,0,1:T(8,128)(2,1)} async-done(((bf16[1024,3,256]{2,0,1:T(8,128)(2,1)}), bf16[128,3,256]{2,0,1:T(8,128)(2,1)}) %reduce-scatter.65.cloned.1.call-update) | async-done | bytes 196624 | tf_op jit(solution)/shard_map/reduce_scatter | solution.py:274
  1755.2 34.6 %reduce-scatter.63.cloned.1.call-done = bf16[128,3,256]{2,0,1:T(8,128)(2,1)} async-done(((bf16[1024,3,256]{2,0,1:T(8,128)(2,1)}), bf16[128,3,256]{2,0,1:T(8,128)(2,1)}) %reduce-scatter.63.cloned.1.call-update) | async-done | bytes 196624 | tf_op jit(solution)/shard_map/reduce_scatter | solution.py:274
  1835.6 37.6 %all-reduce = (f32[261]{0:T(512)}, f32[261]{0:T(512)}) all-reduce(f32[261]{0:T(512)S(1)} %get-tuple-element.115, f32[261]{0:T(512)S(1)} %get-tuple-element.117), channel_id=1, replica_groups=mesh['dp'=8,'mp'=4] {'dp','mp'}, use_global_device_ids=true, to_apply=%region_79.80 | all-reduce | flops 522 | bytes 4176 | tf_op jit(solution)/shard_map/psum | solution.py:509
  1874.3 49.8 %reduce-scatter.85.cloned.1.call-done = f32[32,6]{1,0:T(8,128)} async-done(((f32[1024,6]{1,0:T(8,128)}), f32[32,6]{1,0:T(8,128)}) %reduce-scatter.85.cloned.1.call-update) | async-done | bytes 784
  1925.5 130.8 %reduce-scatter.83.cloned.1.call-done = f32[32,6]{1,0:T(8,128)} async-done(((f32[1024,6]{1,0:T(8,128)}), f32[32,6]{1,0:T(8,128)}) %reduce-scatter.83.cloned.1.call-update) | async-done | bytes 784
  2057.6 97.4 %reduce-scatter.81.cloned.1.call-done = f32[32,261]{1,0:T(8,128)} async-done(((f32[1024,261]{1,0:T(8,128)}), f32[32,261]{1,0:T(8,128)}) %reduce-scatter.81.cloned.1.call-update) | async-done | bytes 33424
  2155.1 101.9 %reduce-scatter.79.cloned.1.call-done = f32[32,261]{1,0:T(8,128)} async-done(((f32[1024,261]{1,0:T(8,128)}), f32[32,261]{1,0:T(8,128)}) %reduce-scatter.79.cloned.1.call-update) | async-done | bytes 33424
  2257.0 143.0 %reduce-scatter.61.cloned.1.call-done = f32[1024,32]{0,1:T(8,128)} async-done(((f32[1024,1024]{0,1:T(8,128)}), f32[1024,32]{0,1:T(8,128)}) %reduce-scatter.61.cloned.1.call-update) | async-done | bytes 131088 | tf_op jit(solution)/shard_map/reduce_scatter | solution.py:505
  2400.0 142.7 %reduce-scatter.59.cloned.1.call-done = f32[1024,32]{0,1:T(8,128)} async-done(((f32[1024,1024]{0,1:T(8,128)}), f32[1024,32]{0,1:T(8,128)}) %reduce-scatter.59.cloned.1.call-update) | async-done | bytes 131088 | tf_op jit(solution)/shard_map/reduce_scatter | solution.py:504
  2542.7 142.6 %reduce-scatter.57.cloned.1.call-done = f32[1024,32]{0,1:T(8,128)} async-done(((f32[1024,1024]{0,1:T(8,128)}), f32[1024,32]{0,1:T(8,128)}) %reduce-scatter.57.cloned.1.call-update) | async-done | bytes 131088 | tf_op jit(solution)/shard_map/reduce_scatter | solution.py:503
  2685.3 142.5 %reduce-scatter.55.cloned.1.call-done = f32[1024,32]{0,1:T(8,128)} async-done(((f32[1024,1024]{0,1:T(8,128)}), f32[1024,32]{0,1:T(8,128)}) %reduce-scatter.55.cloned.1.call-update) | async-done | bytes 131088 | tf_op jit(solution)/shard_map/reduce_scatter | solution.py:500
  (530 shorter events, 824.4 us)
Async XLA Ops:
  7.2 139.2 %all-gather.31.cloned.1.call-start = ((), (), s32[]{:S(2)}) async-start(), calls=%async_computation.26 | async-start | bytes 2162688 | tf_op jit(solution)/shard_map/all_gather | solution.py:110
  7.9 350.6 %all-gather.33.cloned.1.call-start = ((), (), s32[]{:S(2)}) async-start(), calls=%async_computation.27 | async-start | bytes 2621440 | tf_op jit(solution)/shard_map/all_gather | solution.py:57
  149.7 267.9 %all-gather.35.cloned.1.call-start = ((), (), s32[]{:S(2)}) async-start(), calls=%async_computation.29 | async-start | bytes 2162688 | tf_op jit(solution)/shard_map/all_gather | solution.py:113
  150.5 298.0 %reduce-scatter.35.cloned.1.call-start = ((), (), s32[]{:S(2)}) async-start(), calls=%async_computation.28 | async-start | bytes 2621440 | tf_op jit(solution)/shard_map/reduce_scatter | solution.py:65
  415.3 92.7 %all-gather.37.cloned.1.call-start = ((), (), s32[]{:S(2)}) async-start(), calls=%async_computation.30 | async-start | bytes 2162688 | tf_op jit(solution)/shard_map/all_gather | solution.py:114
  415.9 150.5 %all-gather.39.cloned.1.call-start = ((), (), s32[]{:S(2)}) async-start(), calls=%async_computation.31 | async-start | bytes 2162688 | tf_op jit(solution)/shard_map/all_gather | solution.py:115
  416.5 178.7 %all-gather.59.cloned.1.call-start = ((), (), s32[]{:S(2)}) async-start(), calls=%async_computation.62 | async-start | bytes 1769472 | tf_op jit(solution)/shard_map/all_gather | solution.py:123
  417.3 214.4 %all-gather.41.cloned.1.call-start = ((), (), s32[]{:S(2)}) async-start(), calls=%async_computation.32 | async-start | bytes 2621440 | tf_op jit(solution)/shard_map/all_gather | solution.py:57
  570.4 118.1 %reduce-scatter.37.cloned.1.call-start = ((), (), s32[]{:S(2)}) async-start(), calls=%async_computation.33 | async-start | bytes 2621440 | tf_op jit(solution)/shard_map/reduce_scatter | solution.py:65
  732.6 100.5 %all-gather.45.cloned.1.call-start = ((), (), s32[]{:S(2)}) async-start(), calls=%async_computation.36 | async-start | bytes 2621440 | tf_op jit(solution)/shard_map/all_gather | solution.py:57
  769.9 123.6 %reduce-scatter.41.cloned.1.call-start = ((), (), s32[]{:S(2)}) async-start(), calls=%async_computation.37 | async-start | bytes 2621440 | tf_op jit(solution)/shard_map/reduce_scatter | solution.py:65
  897.3 113.4 %reduce-scatter.45.cloned.1.call-start = ((), (), s32[]{:S(2)}) async-start(), calls=%async_computation.41 | async-start | bytes 2621440 | tf_op jit(solution)/shard_map/reduce_scatter | solution.py:74
  979.0 111.3 %all-gather.51.cloned.1.call-start = ((), (), s32[]{:S(2)}) async-start(), calls=%async_computation.42 | async-start | bytes 2621440 | tf_op jit(solution)/shard_map/all_gather | solution.py:61
  1054.8 123.5 %reduce-scatter.47.cloned.1.call-start = ((), (), s32[]{:S(2)}) async-start(), calls=%async_computation.43 | async-start | bytes 2621440 | tf_op jit(solution)/shard_map/reduce_scatter | solution.py:74
  1267.6 114.9 %reduce-scatter.51.cloned.1.call-start = ((), (), s32[]{:S(2)}) async-start(), calls=%async_computation.47 | async-start | bytes 2621440 | tf_op jit(solution)/shard_map/reduce_scatter | solution.py:74
  1395.5 181.1 %reduce-scatter.53.cloned.1.call-start = ((), (), s32[]{:S(2)}) async-start(), calls=%async_computation.49 | async-start | bytes 2621440 | tf_op jit(solution)/shard_map/reduce_scatter | solution.py:74
  1494.5 111.9 %reduce-scatter.77.cloned.1.call-start = ((), (), s32[]{:S(2)}) async-start(), calls=%async_computation.61 | async-start | bytes 589824 | tf_op jit(solution)/shard_map/reduce_scatter | solution.py:283
  1497.7 108.7 %reduce-scatter.75.cloned.1.call-start = ((), (), s32[]{:S(2)}) async-start(), calls=%async_computation.60 | async-start | bytes 589824 | tf_op jit(solution)/shard_map/reduce_scatter | solution.py:283
  1501.4 124.5 %reduce-scatter.73.cloned.1.call-start = ((), (), s32[]{:S(2)}) async-start(), calls=%async_computation.59 | async-start | bytes 589824 | tf_op jit(solution)/shard_map/reduce_scatter | solution.py:280
  1504.7 152.5 %reduce-scatter.71.cloned.1.call-start = ((), (), s32[]{:S(2)}) async-start(), calls=%async_computation.58 | async-start | bytes 589824 | tf_op jit(solution)/shard_map/reduce_scatter | solution.py:280
  1508.0 181.2 %reduce-scatter.69.cloned.1.call-start = ((), (), s32[]{:S(2)}) async-start(), calls=%async_computation.57 | async-start | bytes 589824 | tf_op jit(solution)/shard_map/reduce_scatter | solution.py:277
  1511.4 209.2 %reduce-scatter.67.cloned.1.call-start = ((), (), s32[]{:S(2)}) async-start(), calls=%async_computation.56 | async-start | bytes 589824 | tf_op jit(solution)/shard_map/reduce_scatter | solution.py:277
  1514.8 240.4 %reduce-scatter.65.cloned.1.call-start = ((), (), s32[]{:S(2)}) async-start(), calls=%async_computation.55 | async-start | bytes 1769472 | tf_op jit(solution)/shard_map/reduce_scatter | solution.py:274
  1519.6 270.2 %reduce-scatter.63.cloned.1.call-start = ((), (), s32[]{:S(2)}) async-start(), calls=%async_computation.54 | async-start | bytes 1769472 | tf_op jit(solution)/shard_map/reduce_scatter | solution.py:274
  1525.5 398.6 %reduce-scatter.85.cloned.1.call-start = ((), (), s32[]{:S(2)}) async-start(), calls=%async_computation.67 | async-start | bytes 540672
  1580.5 475.8 %reduce-scatter.83.cloned.1.call-start = ((), (), s32[]{:S(2)}) async-start(), calls=%async_computation.66 | async-start | bytes 540672
  1582.4 572.7 %reduce-scatter.81.cloned.1.call-start = ((), (), s32[]{:S(2)}) async-start(), calls=%async_computation.65 | async-start | bytes 1622016
  1588.2 668.8 %reduce-scatter.79.cloned.1.call-start = ((), (), s32[]{:S(2)}) async-start(), calls=%async_computation.64 | async-start | bytes 1622016
  1589.9 810.1 %reduce-scatter.61.cloned.1.call-start = ((), (), s32[]{:S(2)}) async-start(), calls=%async_computation.53 | async-start | bytes 4325376 | tf_op jit(solution)/shard_map/reduce_scatter | solution.py:505
  1594.1 948.6 %reduce-scatter.59.cloned.1.call-start = ((), (), s32[]{:S(2)}) async-start(), calls=%async_computation.52 | async-start | bytes 4325376 | tf_op jit(solution)/shard_map/reduce_scatter | solution.py:504
  1598.3 1087.0 %reduce-scatter.57.cloned.1.call-start = ((), (), s32[]{:S(2)}) async-start(), calls=%async_computation.51 | async-start | bytes 4325376 | tf_op jit(solution)/shard_map/reduce_scatter | solution.py:503
  1602.5 1225.3 %reduce-scatter.55.cloned.1.call-start = ((), (), s32[]{:S(2)}) async-start(), calls=%async_computation.50 | async-start | bytes 4325376 | tf_op jit(solution)/shard_map/reduce_scatter | solution.py:500
  (124 other events, 7396.6 us)
Sparse Core Ops, SparseCore 0:
  10.9 59.2 all-gather.30
  149.8 37.2 all-gather.32
  190.0 57.6 all-gather.34
  415.4 33.0 reduce-scatter.34
  451.6 56.3 all-gather.36
  511.2 55.2 all-gather.38
  597.7 33.9 all-gather.40
  653.2 35.1 reduce-scatter.36
  691.2 35.2 all-gather.42
  732.1 35.1 reduce-scatter.38
  798.9 34.0 all-gather.44
  858.2 35.1 reduce-scatter.40
  896.9 35.2 all-gather.46
  933.9 35.2 all-gather.48
  975.5 35.1 reduce-scatter.44
  1013.9 35.1 reduce-scatter.42
  1054.9 35.2 all-gather.50
  1143.1 35.1 reduce-scatter.46
  1185.8 35.2 all-gather.52
  1226.6 35.1 reduce-scatter.48
  1267.7 35.2 all-gather.54
  1347.2 35.1 reduce-scatter.50
  1395.6 35.2 all-gather.56
  1494.6 35.1 reduce-scatter.52
  1792.1 131.9 reduce-scatter.84
  1926.3 129.9 reduce-scatter.82
  2061.9 93.1 reduce-scatter.80
  2160.9 96.0 reduce-scatter.78
  2259.7 140.2 reduce-scatter.60
  2402.8 139.8 reduce-scatter.58
  2545.6 139.7 reduce-scatter.56
  2688.2 139.5 reduce-scatter.54
  (10 shorter events, 293.8 us)
where the time goes:
time: 2840 us; the launch traced here: 2830 us
  waiting for transfers between devices  1830 us (64%)
  blocking collectives  430 us (15%)
  matrix products  365 us (13%)
  other arithmetic  96.7 us (3%)
  local copies, waits for them, and re-layouts  93 us (3%)
    unnamed x46, waiting for transfers between devices  384 us
    all_gather x5, waiting for transfers between devices, gather_grads(): return lax.all_gather(payload, 'mp', axis=0, tiled=True)  175 us
    reduce_scatter x5, waiting for transfers between devices, sum_branch(): lax.psum_scatter(row_term(jnp.int32(0), own_rows * lax.axis_size('mp')).a...  172 us
    reduce_scatter x1, waiting for transfers between devices, shards(): lax.psum_scatter(cross_down_grad, ('dp', 'mp'), scatter_dimension=1, tile...  143 us
    reduce_scatter x1, waiting for transfers between devices, shards(): lax.psum_scatter(cross_up_grad, ('dp', 'mp'), scatter_dimension=1, tiled=...  143 us
    reduce_scatter x1, waiting for transfers between devices, shards(): lax.psum_scatter(cross_out_grad, ('dp', 'mp'), scatter_dimension=1, tiled...  143 us
    reduce_scatter x1, waiting for transfers between devices, shards(): lax.psum_scatter(cross_query_grad, ('dp', 'mp'), scatter_dimension=1, til...  142 us
    reduce_scatter x5, waiting for transfers between devices, sum_inputs(): lax.psum_scatter(row_term(jnp.int32(0), own_rows * lax.axis_size('mp')).a...  137 us
  transfers between devices with their start and end apart: 42, of which 36 were waited for; matrix products, arithmetic and copies ran while one was open for 10% of the time, Pallas kernels for 0%

commit v1 on v0

--- a/solution.py
+++ b/solution.py
@@ -1,8 +1,11 @@
+import functools
 import math
 
 import jax
 import jax.numpy as jnp
 from jax import lax
+from jax.experimental import pallas as pl
+from jax.experimental.pallas import tpu as pltpu
 from jax.sharding import PartitionSpec as P
 
 HD = 128
@@ -528,9 +531,1014 @@
     )
 
 
+MESH_ID = pl.DeviceIdType.MESH
+ANY = pl.BlockSpec(memory_space=pl.ANY)
+DMA = pltpu.SemaphoreType.DMA
+
+
+def place():
+    dp = lax.axis_index("dp")
+    mp = lax.axis_index("mp")
+    return dp, mp, dp // 2, dp % 2, mp // 2, mp % 2
+
+
+def greet(targets):
+    barrier = pltpu.get_barrier_semaphore()
+    for device, condition in targets:
+
+        def signal(device=device):
+            pl.semaphore_signal(barrier, inc=1, device_id=device, device_id_type=MESH_ID)
+
+        if condition is None:
+            signal()
+        else:
+            pl.when(condition)(signal)
+    fixed = sum(1 for _, condition in targets if condition is None)
+    varying = [condition.astype(jnp.int32) for _, condition in targets if condition is not None]
+    pl.semaphore_wait(barrier, sum(varying, fixed))
+
+
+def remote(source, target, send, recv, device):
+    return pltpu.make_async_remote_copy(
+        src_ref=source,
+        dst_ref=target,
+        send_sem=send,
+        recv_sem=recv,
+        device_id=device,
+        device_id_type=MESH_ID,
+    )
+
+
+def when(condition, action):
+    if condition is None:
+        action()
+    else:
+        pl.when(condition)(action)
+
+
+def both(first, second):
+    if first is None:
+        return second
+    if second is None:
+        return first
+    return jnp.logical_and(first, second)
+
+
+class Gatherer:
+    def __init__(self, line, slabs, outs, by_mp, sems):
+        self.line = line
+        self.slabs = slabs
+        self.outs = outs
+        self.by_mp = by_mp
+        (
+            self.own_sem,
+            self.line_send,
+            self.line_recv,
+            self.plane_send,
+            self.plane_recv,
+            self.pass_send,
+            self.pass_recv,
+            self.core_send,
+            self.core_recv,
+        ) = sems
+        self.dp, self.mp, self.z, self.core, self.y, self.x = place()
+
+    @staticmethod
+    def sem_shapes(chunks, line):
+        return [
+            DMA((chunks,)),
+            DMA((chunks, line, 2)),
+            DMA((chunks, line)),
+            DMA((chunks, line, 2)),
+            DMA((chunks, line, 2)),
+            DMA((chunks, line, 2)),
+            DMA((chunks, line, 2)),
+            DMA((chunks, line, 4)),
+            DMA((chunks, line, 4)),
+        ]
+
+    def partners(self):
+        z = self.z
+        return [
+            ((self.dp + 2, self.mp), z < self.line - 1),
+            ((self.dp - 2, self.mp), z > 0),
+            ((self.dp, self.mp ^ 1), None),
+            ((self.dp, self.mp ^ 2), None),
+            ((self.dp ^ 1, self.mp), None),
+        ]
+
+    def slot(self, chunk, z, core, mp):
+        out = self.outs[chunk]
+        return out.at[mp, 2 * z + core] if self.by_mp[chunk] else out.at[2 * z + core, mp]
+
+    def halves(self, ref):
+        rows = ref.shape[0] // 2
+        return ref.at[pl.ds(0, rows)], ref.at[pl.ds(rows, rows)]
+
+    def line_copy(self, chunk, z, way, source=None):
+        slot = self.slot(chunk, z, self.core, self.mp)
+        step = 2 if way == 0 else -2
+        return remote(
+            slot if source is None else source,
+            slot,
+            self.line_send.at[chunk, z, way],
+            self.line_recv.at[chunk, z],
+            (self.dp + step, self.mp),
+        )
+
+    def plane_copy(self, chunk, z, way, source=None):
+        slot = self.slot(chunk, z, self.core, self.mp)
+        return remote(
+            slot if source is None else source,
+            slot,
+            self.plane_send.at[chunk, z, way],
+            self.plane_recv.at[chunk, z, way],
+            (self.dp, self.mp ^ (1 if way == 0 else 2)),
+        )
+
+    def pass_copy(self, chunk, z, way):
+        slot = self.slot(chunk, z, self.core, self.mp ^ (1 if way == 0 else 2))
+        half = self.halves(slot)[way]
+        return remote(
+            half,
+            half,
+            self.pass_send.at[chunk, z, way],
+            self.pass_recv.at[chunk, z, way],
+            (self.dp, self.mp ^ (2 if way == 0 else 1)),
+        )
+
+    def core_copy(self, chunk, z, mp, turn):
+        slot = self.slot(chunk, z, self.core, mp)
+        return remote(
+            slot,
+            slot,
+            self.core_send.at[chunk, z, turn],
+            self.core_recv.at[chunk, z, turn],
+            (self.dp ^ 1, self.mp),
+        )
+
+    def arrivals(self):
+        z = self.z
+        order = [(z, None, None)]
+        for distance in range(1, self.line):
+            order.append((z - distance, z >= distance, 0))
+            order.append((z + distance, z + distance < self.line, 1))
+        return order
+
+    def own_copy(self, chunk):
+        return pltpu.make_async_copy(
+            self.slabs[chunk], self.slot(chunk, self.z, self.core, self.mp), self.own_sem.at[chunk]
+        )
+
+    def can_pass(self, way):
+        return self.z < self.line - 1 if way == 0 else self.z > 0
+
+    def begin(self, chunk):
+        self.own_copy(chunk).start()
+        slab = self.slabs[chunk]
+        for way in (0, 1):
+            when(
+                self.can_pass(way),
+                lambda way=way: self.line_copy(chunk, self.z, way, slab).start(),
+            )
+        for way in (0, 1):
+            self.plane_copy(chunk, self.z, way, slab).start()
+
+    def stage_line(self, chunk, turn):
+        if turn == 0:
+            self.begin(chunk)
+            return
+        z, condition, way = self.arrivals()[turn]
+
+        def act():
+            self.line_copy(chunk, z, way).wait_recv()
+            when(self.can_pass(way), lambda: self.line_copy(chunk, z, way).start())
+            for plane_way in (0, 1):
+                self.plane_copy(chunk, z, plane_way).start()
+
+        when(condition, act)
+
+    def stage_plane(self, chunk, turn):
+        z, condition, _ = self.arrivals()[turn]
+
+        def act():
+            for way in (0, 1):
+                self.plane_copy(chunk, z, way).wait_recv()
+                self.pass_copy(chunk, z, way).start()
+            if turn == 0:
+                self.own_copy(chunk).wait()
+            self.core_copy(chunk, z, self.mp, 0).start()
+            self.core_copy(chunk, z, self.mp ^ 1, 1).start()
+            self.core_copy(chunk, z, self.mp ^ 2, 2).start()
+
+        when(condition, act)
+
+    def stage_pass(self, chunk, turn):
+        z, condition, _ = self.arrivals()[turn]
+
+        def act():
+            for way in (0, 1):
+                self.pass_copy(chunk, z, way).wait_recv()
+            self.core_copy(chunk, z, self.mp ^ 3, 3).start()
+
+        when(condition, act)
+
+    def stage_core(self, chunk, turn):
+        z, condition, _ = self.arrivals()[turn]
+
+        def act():
+            for piece in range(4):
+                self.core_copy(chunk, z, self.mp, piece).wait_recv()
+
+        when(condition, act)
+
+    def drain(self, chunk):
+        for turn, (z, condition, way) in enumerate(self.arrivals()):
+
+            def act(turn=turn, z=z, way=way):
+                if turn == 0:
+                    for own_way in (0, 1):
+                        when(
+                            self.can_pass(own_way),
+                            lambda own_way=own_way: self.line_copy(
+                                chunk, z, own_way, self.slabs[chunk]
+                            ).wait_send(),
+                        )
+                else:
+                    when(self.can_pass(way), lambda: self.line_copy(chunk, z, way).wait_send())
+                for plane_way in (0, 1):
+                    self.plane_copy(chunk, z, plane_way).wait_send()
+                    self.pass_copy(chunk, z, plane_way).wait_send()
+                for piece in range(4):
+                    self.core_copy(chunk, z, self.mp, piece).wait_send()
+
+            when(condition, act)
+
+    def steps(self, chunks, lag=2):
+        turns = 2 * self.line - 1
+        units = [(chunk, turn) for chunk in chunks for turn in range(turns)]
+        todo = []
+        for at in range(len(units) + 3 * lag):
+            for stage, late in (
+                (self.stage_line, 0),
+                (self.stage_plane, lag),
+                (self.stage_pass, 2 * lag),
+                (self.stage_core, 3 * lag),
+            ):
+                if 0 <= at - late < len(units):
+                    todo.append(functools.partial(stage, *units[at - late]))
+        for chunk in chunks:
+            todo.append(functools.partial(self.drain, chunk))
+        return todo
+
+
+def gather_all(slabs, by_mp, line):
+    count = len(slabs)
+
+    def kernel(*refs):
+        ins, outs, sems = refs[:count], refs[count : 2 * count], refs[2 * count :]
+        gatherer = Gatherer(line, ins, outs, by_mp, sems)
+        greet(gatherer.partners())
+        for step in gatherer.steps(range(count)):
+            step()
+
+    shapes = tuple(
+        jax.ShapeDtypeStruct(
+            ((4, 2 * line) if over_mp else (2 * line, 4)) + slab.shape, slab.dtype
+        )
+        for slab, over_mp in zip(slabs, by_mp)
+    )
+    return pl.pallas_call(
+        kernel,
+        out_shape=shapes,
+        in_specs=[ANY] * count,
+        out_specs=[ANY] * count,
+        scratch_shapes=Gatherer.sem_shapes(count, line),
+        compiler_params=pltpu.CompilerParams(collective_id=0, has_side_effects=True),
+        name="weight_gather",
+    )(*slabs)
+
+
+class Reducer:
+    def __init__(self, line, parts, outs, by_mp, scratch):
+        self.line = line
+        self.parts = parts
+        self.outs = outs
+        self.by_mp = by_mp
+        count = len(parts)
+        self.core_in = scratch[:count]
+        self.own_in = scratch[count : 2 * count]
+        self.pass_in = scratch[2 * count : 3 * count]
+        self.plane_in = scratch[3 * count : 4 * count]
+        self.line_in = scratch[4 * count : 5 * count]
+        (
+            self.own_sem,
+            self.core_send,
+            self.core_recv,
+            self.pass_send,
+            self.pass_recv,
+            self.plane_send,
+            self.plane_recv,
+            self.line_send,
+            self.line_recv,
+        ) = scratch[5 * count :]
+        self.dp, self.mp, self.z, self.core, self.y, self.x = place()
+
+    @staticmethod
+    def scratch_shapes(slabs, line):
+        def buffers(lead, halve=False):
+            return [
+                pltpu.VMEM(
+                    lead + ((rows // 2 if halve else rows), cols), jnp.bfloat16
+                )
+                for rows, cols in slabs
+            ]
+
+        chunks = len(slabs)
+        return (
+            buffers((line, 4))
+            + buffers((4,))
+            + buffers((line, 2), True)
+            + buffers((line, 2))
+            + buffers((line, 2))
+            + [
+                DMA((chunks, 4)),
+                DMA((chunks, line, 4)),
+                DMA((chunks, line, 4)),
+                DMA((chunks, line, 2)),
+                DMA((chunks, line, 2)),
+                DMA((chunks, line, 2)),
+                DMA((chunks, line, 2)),
+                DMA((chunks, line, 2)),
+                DMA((chunks, line, 2)),
+            ]
+        )
+
+    partners = Gatherer.partners
+    halves = Gatherer.halves
+
+    def part(self, chunk, z, core, mp):
+        part = self.parts[chunk]
+        return part.at[mp, 2 * z + core] if self.by_mp[chunk] else part.at[2 * z + core, mp]
+
+    def core_copy(self, chunk, z, mp):
+        return remote(
+            self.part(chunk, z, 1 - self.core, mp),
+            self.core_in[chunk].at[z, mp],
+            self.core_send.at[chunk, z, mp],
+            self.core_recv.at[chunk, z, mp],
+            (self.dp ^ 1, self.mp),
+        )
+
+    def own_copy(self, chunk, z, mp):
+        return pltpu.make_async_copy(
+            self.part(chunk, z, self.core, mp),
+            self.own_in[chunk].at[mp],
+            self.own_sem.at[chunk, mp],
+        )
+
+    def pass_copy(self, chunk, z, way):
+        half = self.halves(self.core_in[chunk].at[z, self.mp ^ 3])[way]
+        return remote(
+            half,
+            self.pass_in[chunk].at[z, way],
+            self.pass_send.at[chunk, z, way],
+            self.pass_recv.at[chunk, z, way],
+            (self.dp, self.mp ^ (2 if way == 0 else 1)),
+        )
+
+    def plane_copy(self, chunk, z, way):
+        mate = self.mp ^ (1 if way == 0 else 2)
+        return remote(
+            self.core_in[chunk].at[z, mate],
+            self.plane_in[chunk].at[z, way],
+            self.plane_send.at[chunk, z, way],
+            self.plane_recv.at[chunk, z, way],
+            (self.dp, mate),
+        )
+
+    def line_copy(self, chunk, z, way):
+        return remote(
+            self.core_in[chunk].at[z, self.mp],
+            self.line_in[chunk].at[z, way],
+            self.line_send.at[chunk, z, way],
+            self.line_recv.at[chunk, z, way],
+            (self.dp + (-2 if way == 0 else 2), self.mp),
+        )
+
+    @staticmethod
+    def add(target, sources, result=None):
+        rows = target.shape[0]
+        step = 16
+
+        def body(turn, carry):
+            at = pl.ds(pl.multiple_of(turn * step, step), step)
+            total = target[at, :].astype(jnp.float32)
+            for source in sources:
+                total = total + source[at, :].astype(jnp.float32)
+            if result is None:
+                target[at, :] = total.astype(jnp.bfloat16)
+            else:
+                result[at, :] = total
+            return carry
+
+        lax.fori_loop(0, rows // step, body, 0)
+
+    def order(self):
+        low, high, found = 0, self.line - 1, []
+        while low <= high:
+            found.append(low)
+            if high != low:
+                found.append(high)
+            low, high = low + 1, high - 1
+        return found
+
+    def stage_begin(self, chunk, z):
+        for mp in range(4):
+            self.core_copy(chunk, z, mp).start()
+
+    def stage_core(self, chunk, z):
+        for mp in range(4):
+            self.own_copy(chunk, z, mp).start()
+        for mp in range(4):
+            self.core_copy(chunk, z, mp).wait_recv()
+            self.own_copy(chunk, z, mp).wait()
+            self.add(self.core_in[chunk].at[z, mp], [self.own_in[chunk].at[mp]])
+        for way in (0, 1):
+            self.pass_copy(chunk, z, way).start()
+
+    def stage_pass(self, chunk, z):
+        for way in (0, 1):
+            self.pass_copy(chunk, z, way).wait_recv()
+            mate = self.mp ^ (1 if way == 0 else 2)
+            self.add(
+                self.halves(self.core_in[chunk].at[z, mate])[way],
+                [self.pass_in[chunk].at[z, way]],
+            )
+            self.plane_copy(chunk, z, way).start()
+
+    def stage_plane(self, chunk, z):
+        for way in (0, 1):
+            self.plane_copy(chunk, z, way).wait_recv()
+        self.add(
+            self.core_in[chunk].at[z, self.mp],
+            [self.plane_in[chunk].at[z, 0], self.plane_in[chunk].at[z, 1]],
+        )
+        last = self.line - 1
+        if z < last:
+            when(self.z == last, lambda: self.line_copy(chunk, z, 0).start())
+        if z > 0:
+            when(self.z == 0, lambda: self.line_copy(chunk, z, 1).start())
+
+    def stage_line(self, chunk, z):
+        last = self.line - 1
+        mine = self.core_in[chunk].at[z, self.mp]
+
+        def join(way):
+            self.line_copy(chunk, z, way).wait_recv()
+            self.add(mine, [self.line_in[chunk].at[z, way]])
+            self.line_copy(chunk, z, way).start()
+
+        when(jnp.logical_and(self.z > z, self.z < last), lambda: join(0))
+        when(jnp.logical_and(self.z < z, self.z > 0), lambda: join(1))
+
+        def finish():
+            sources = []
+            if z < last:
+                self.line_copy(chunk, z, 0).wait_recv()
+                sources.append(self.line_in[chunk].at[z, 0])
+            if z > 0:
+                self.line_copy(chunk, z, 1).wait_recv()
+                sources.append(self.line_in[chunk].at[z, 1])
+            self.add(mine, sources, self.outs[chunk])
+
+        when(self.z == z, finish)
+
+    def drain(self, chunk, z):
+        for mp in range(4):
+            self.core_copy(chunk, z, mp).wait_send()
+        for way in (0, 1):
+            self.pass_copy(chunk, z, way).wait_send()
+            self.plane_copy(chunk, z, way).wait_send()
+        when(self.z > z, lambda: self.line_copy(chunk, z, 0).wait_send())
+        when(self.z < z, lambda: self.line_copy(chunk, z, 1).wait_send())
+
+    def steps(self, chunks, lag=1):
+        units = [(chunk, z) for chunk in chunks for z in self.order()]
+        todo = [functools.partial(self.stage_begin, *unit) for unit in units]
+        for at in range(len(units) + 3 * lag):
+            for stage, late in (
+                (self.stage_core, 0),
+                (self.stage_pass, lag),
+                (self.stage_plane, 2 * lag),
+                (self.stage_line, 3 * lag),
+            ):
+                if 0 <= at - late < len(units):
+                    todo.append(functools.partial(stage, *units[at - late]))
+        for unit in units:
+            todo.append(functools.partial(self.drain, *unit))
+        return todo
+
+
+def reduce_all(parts, by_mp, line):
+    count = len(parts)
+    slabs = [part.shape[2:] for part in parts]
+
+    def kernel(*refs):
+        ins, outs, scratch = refs[:count], refs[count : 2 * count], refs[2 * count :]
+        reducer = Reducer(line, ins, outs, by_mp, scratch)
+        greet(reducer.partners())
+        for step in reducer.steps(range(count)):
+            step()
+
+    return pl.pallas_call(
+        kernel,
+        out_shape=tuple(jax.ShapeDtypeStruct(slab, jnp.float32) for slab in slabs),
+        in_specs=[ANY] * count,
+        out_specs=[pl.BlockSpec(memory_space=pltpu.VMEM)] * count,
+        scratch_shapes=Reducer.scratch_shapes(slabs, line),
+        compiler_params=pltpu.CompilerParams(
+            collective_id=1, has_side_effects=True, vmem_limit_bytes=60 * 1024 * 1024
+        ),
+        name="grad_reduce",
+    )(*parts)
+
+
+def exchange(arrays, kind, collective_id):
+    count = len(arrays)
+    sources = {"mp": 4, "mp_split": 4, "to_work": 4, "from_work": 4}[kind]
+
+    def kernel(*refs):
+        ins, outs = refs[:count], refs[count : 2 * count]
+        own_sem, send_sem, recv_sem = refs[2 * count :]
+        dp, mp, z, core, y, x = place()
+        greet(
+            [
+                ((dp ^ flip_core, mp ^ flip_mp), None)
+                for flip_core in (0, 1)
+                for flip_mp in range(4)
+                if flip_core or flip_mp
+            ]
+        )
+        todo = []
+        for at in range(count):
+            for turn in range(4):
+                if kind == "mp":
+                    peer = mp ^ turn
+                    device, slot, piece, frm = (dp, peer), mp, ins[at], peer
+                elif kind == "mp_split":
+                    peer = mp ^ turn
+                    device, slot, piece, frm = (dp, peer), mp, ins[at].at[peer], peer
+                elif kind == "to_work":
+                    device = (2 * z + turn % 2, 2 * core + turn // 2)
+                    slot, piece, frm = mp, ins[at].at[turn], turn
+                else:
+                    device = (2 * z + mp // 2, turn)
+                    slot, piece, frm = 2 * (mp % 2) + core, ins[at], turn
+                here = jnp.logical_and(device[0] == dp, device[1] == mp)
+                todo.append((at, turn, device, slot, piece, frm, here))
+        for at, turn, device, slot, piece, frm, here in todo:
+            out = outs[at].at[slot]
+            when(
+                jnp.logical_not(here),
+                lambda: remote(
+                    piece, out, send_sem.at[at, turn], recv_sem.at[at, slot], device
+                ).start(),
+            )
+            when(here, lambda: pltpu.make_async_copy(piece, out, own_sem.at[at]).start())
+        for at, turn, device, slot, piece, frm, here in todo:
+            out = outs[at].at[slot]
+            when(
+                jnp.logical_not(here),
+                lambda: remote(
+                    piece, out, send_sem.at[at, turn], recv_sem.at[at, slot], device
+                ).wait_send(),
+            )
+            when(here, lambda: pltpu.make_async_copy(piece, out, own_sem.at[at]).wait())
+        for at in range(count):
+            for slot in range(4):
+                if kind in ("mp", "mp_split"):
+                    self_slot = mp == slot
+                elif kind == "to_work":
+                    self_slot = jnp.logical_and(mp // 2 == core, mp == slot)
+                else:
+                    self_slot = jnp.logical_and(
+                        2 * core + slot // 2 == mp, slot % 2 == core
+                    )
+                out = outs[at].at[slot]
+                piece = ins[at] if kind in ("mp", "from_work") else ins[at].at[0]
+                when(
+                    jnp.logical_not(self_slot),
+                    lambda: remote(
+                        piece, out, send_sem.at[at, 0], recv_sem.at[at, slot], (dp, mp)
+                    ).wait_recv(),
+                )
+
+    shapes = tuple(
+        jax.ShapeDtypeStruct(
+            (4,) + (a.shape if kind in ("mp", "from_work") else a.shape[1:]), a.dtype
+        )
+        for a in arrays
+    )
+    return pl.pallas_call(
+        kernel,
+        out_shape=shapes,
+        in_specs=[ANY] * count,
+        out_specs=[ANY] * count,
+        scratch_shapes=[DMA((count,)), DMA((count, 4)), DMA((count, 4))],
+        compiler_params=pltpu.CompilerParams(collective_id=collective_id, has_side_effects=True),
+        name="exchange_" + kind,
+    )(*arrays)
+
+
+def work_moves(line):
+    pairs = []
+    for dp in range(2 * line):
+        for mp in range(4):
+            z, core = dp // 2, dp % 2
+            pairs.append((dp * 4 + mp, (2 * z + mp % 2) * 4 + 2 * core + mp // 2))
+    return pairs
+
+
+def sibling(value, line):
+    pairs = [(dp * 4 + mp, (dp ^ 1) * 4 + mp) for dp in range(2 * line) for mp in range(4)]
+    return lax.ppermute(value, ("dp", "mp"), pairs)
+
+
+def fast_shards(
+    latents,
+    pixels,
+    pixel_counts,
+    cross_query,
+    cross_key,
+    cross_value,
+    cross_out,
+    cross_up,
+    cross_down,
+    block_qkv,
+    block_out,
+    block_up,
+    block_down,
+    norm_gains,
+    norm_biases,
+    pixel_gain,
+    pixel_bias,
+    cotangent,
+):
+    bf16, f32 = jnp.bfloat16, jnp.float32
+    line = lax.axis_size("dp") // 2
+    layers, rows_d, _, cols_m = block_qkv.shape
+    own_rows, width = latents.shape
+    items, slots, channels = pixels.shape
+    own_cols = cross_query.shape[1]
+    scale = 1.0 / math.sqrt(width)
+    moves = work_moves(line)
+    back_moves = [(b, a) for a, b in moves]
+    both_axes = ("dp", "mp")
+    work_latents = lax.ppermute(latents, both_axes, moves)
+    work_cotangent = lax.ppermute(cotangent, both_axes, moves)
+
+    pad = (-channels) % 128
+    wide = channels + pad
+
+    def lanes(v):
+        return jnp.pad(v, ((0, 0), (0, pad)))
+
+    norms = jnp.concatenate([norm_gains, norm_biases], axis=0)
+    norm_count = norm_gains.shape[0]
+    slab_q = jnp.concatenate(
+        [
+            cross_query.T,
+            lanes(cross_key.T),
+            lanes(cross_value.T),
+            jnp.pad(norms.T, ((0, 0), (0, 128 - 2 * norm_count))),
+        ],
+        axis=1,
+    )
+    slab_c = jnp.concatenate([cross_up.T, cross_down.T, cross_out.T], axis=0)
+    slabs_l = [
+        jnp.concatenate(
+            [
+                block_qkv[l].reshape(rows_d, 3 * cols_m),
+                block_out[l],
+                block_up[l],
+                block_down[l],
+            ],
+            axis=1,
+        )
+        for l in range(layers)
+    ]
+    gathered = gather_all(
+        [slab_q, slab_c] + slabs_l, [False, False] + [True] * layers, line
+    )
+    all_q = gathered[0].reshape(width, -1)
+    all_c = gathered[1].reshape(-1, 3, own_cols, width)
+    query_t = all_q[:, :width]
+    key_t = all_q[:, width : width + channels]
+    value_t = all_q[:, width + wide : width + wide + channels]
+    norm_rows = all_q[:, width + 2 * wide : width + 2 * wide + 2 * norm_count].T.astype(f32)
+    gain_rows, bias_rows = norm_rows[:norm_count], norm_rows[norm_count:]
+    up_t = all_c[:, 0].reshape(-1, width)
+    down_t = all_c[:, 1].reshape(-1, width)
+    out_t = all_c[:, 2].reshape(-1, width)
+    layer_w = [g.reshape(4, width, 6 * cols_m) for g in gathered[2:]]
+
+    start_rows = latents.astype(f32)
+    query_in = layer_norm(start_rows, gain_rows[0], bias_rows[0]).astype(bf16)
+    queries = times_transposed(query_in, query_t).astype(bf16)
+    qk = (matmul(queries, key_t) * scale).astype(bf16)
+    (qk_all,) = exchange([lanes(qk)], "mp", 2)
+    half_rows = own_rows
+    qk_all = qk_all.reshape(items, 2 * half_rows, wide)[:, :, :channels]
+    pixel_floats = pixels.astype(f32)
+    pixel_gain_row = pixel_gain.astype(f32)
+    pixel_bias_row = pixel_bias.astype(f32)
+    pixel_in = layer_norm(pixel_floats, pixel_gain_row, pixel_bias_row).astype(bf16)
+    positions = lax.axis_index("mp") * slots + jnp.arange(slots, dtype=jnp.int32)
+    present = positions[None, :] < pixel_counts[:, None]
+
+    def cross_scores():
+        raw = jnp.einsum("iqc,ipc->iqp", qk_all, pixel_in, preferred_element_type=f32)
+        return jnp.where(present[:, None, :], raw, masked_score)
+
+    scores = cross_scores()
+    local_top = jnp.max(scores, axis=-1)
+    lifted = jnp.exp(scores - local_top[:, :, None]) * present.astype(f32)[:, None, :]
+    local_total = jnp.sum(lifted, axis=-1)
+    taken = jnp.einsum("iqp,ipc->iqc", lifted.astype(bf16), pixel_in, preferred_element_type=f32)
+    taken = jnp.pad(taken.astype(bf16), ((0, 0), (0, 0), (0, pad)))
+    stats = jnp.stack([local_top, local_total], axis=1).reshape(items, 2, 2, half_rows)
+    stats = jnp.pad(jnp.swapaxes(stats, 1, 2).reshape(4, 2, half_rows), ((0, 0), (0, 6), (0, 0)))
+    taken_parts, stat_parts = exchange(
+        [taken.reshape(4, half_rows, wide), stats], "to_work", 3
+    )
+    tops, totals = stat_parts[:, 0], stat_parts[:, 1]
+    top = jnp.max(tops, axis=0)
+    shares = jnp.exp(tops - top[None])
+    total = jnp.sum(shares * totals, axis=0)
+    log_total = top + jnp.log(total)
+    px = jnp.sum(taken_parts.astype(f32) * shares[:, :, None], axis=0) / total[:, None]
+    px = px[:, :channels]
+    px_low = px.astype(bf16)
+    context_own = times_transposed(px_low, value_t).astype(bf16)
+    base_rows = work_latents.astype(f32)
+    after_cross = base_rows + times_transposed(context_own, out_t)
+    cross_hidden_in = layer_norm(after_cross, gain_rows[1], bias_rows[1]).astype(bf16)
+    cross_hidden = times_transposed(cross_hidden_in, up_t)
+    cross_active = jax.nn.gelu(cross_hidden).astype(bf16)
+    current = after_cross + times_transposed(cross_active, down_t)
+
+    heads = cols_m // HD
+    block_scale = 1.0 / math.sqrt(HD)
+
+    def split_heads(v):
+        return v.reshape(4, -1, heads, HD)
+
+    saved = []
+    for l in range(layers):
+        w = layer_w[l]
+        w_qkv, w_out, w_up, w_down = (
+            w[:, :, : 3 * cols_m],
+            w[:, :, 3 * cols_m : 4 * cols_m],
+            w[:, :, 4 * cols_m : 5 * cols_m],
+            w[:, :, 5 * cols_m :],
+        )
+        normed = layer_norm(current, gain_rows[2 + 2 * l], bias_rows[2 + 2 * l]).astype(bf16)
+        qkv = jnp.einsum("rd,mdk->mrk", normed, w_qkv, preferred_element_type=f32).astype(bf16)
+        queries_h = split_heads(qkv[:, :, :cols_m])
+        kv = qkv[:, :, cols_m:]
+        kv_all = jnp.concatenate([kv, sibling(kv, line)], axis=1)
+        keys_h = split_heads(kv_all[:, :, :cols_m])
+        values_h = split_heads(kv_all[:, :, cols_m:])
+        raw = (
+            jnp.einsum("mqhe,mkhe->mhqk", queries_h, keys_h, preferred_element_type=f32)
+            * block_scale
+        )
+        row_top = jnp.max(raw, axis=-1, keepdims=True)
+        lifted_h = jnp.exp(raw - row_top)
+        row_total = jnp.sum(lifted_h, axis=-1, keepdims=True)
+        attention = lifted_h / row_total
+        log_h = row_top + jnp.log(row_total)
+        context = jnp.einsum(
+            "mhqk,mkhe->mqhe", attention.astype(bf16), values_h, preferred_element_type=f32
+        )
+        context = context.astype(bf16).reshape(4, own_rows, cols_m)
+        middle = current + jnp.einsum("mrk,mdk->rd", context, w_out, preferred_element_type=f32)
+        hidden_in = layer_norm(middle, gain_rows[3 + 2 * l], bias_rows[3 + 2 * l]).astype(bf16)
+        hidden = jnp.einsum("rd,mdf->mrf", hidden_in, w_up, preferred_element_type=f32)
+        active = jax.nn.gelu(hidden).astype(bf16)
+        result = middle + jnp.einsum("mrf,mdf->rd", active, w_down, preferred_element_type=f32)
+        saved.append(
+            (
+                w_qkv,
+                w_out,
+                w_up,
+                w_down,
+                current,
+                normed,
+                queries_h,
+                keys_h,
+                values_h,
+                log_h,
+                context,
+                middle,
+                hidden_in,
+                hidden,
+                active,
+            )
+        )
+        current = result
+    latents_out = lax.ppermute(current.astype(bf16), both_axes, back_moves)
+
+    gain_parts = [None] * norm_count
+    bias_parts = [None] * norm_count
+    layer_parts = [None] * layers
+    current_cot = work_cotangent.astype(f32)
+    for l in reversed(range(layers)):
+        (
+            w_qkv,
+            w_out,
+            w_up,
+            w_down,
+            current,
+            normed,
+            queries_h,
+            keys_h,
+            values_h,
+            log_h,
+            context,
+            middle,
+            hidden_in,
+            hidden,
+            active,
+        ) = saved[l]
+        down_cot = current_cot.astype(bf16)
+        down_grad = jnp.einsum("rd,mrf->mdf", down_cot, active, preferred_element_type=f32)
+        active_cot = jnp.einsum("rd,mdf->mrf", down_cot, w_down, preferred_element_type=f32)
+        hidden_cot = gelu_back(hidden, active_cot).astype(bf16)
+        up_grad = jnp.einsum("rd,mrf->mdf", hidden_in, hidden_cot, preferred_element_type=f32)
+        hidden_in_cot = jnp.einsum("mrf,mdf->rd", hidden_cot, w_up, preferred_element_type=f32)
+        middle_cot, gain_parts[3 + 2 * l], bias_parts[3 + 2 * l] = norm_back(
+            middle, gain_rows[3 + 2 * l], bias_rows[3 + 2 * l], hidden_in_cot
+        )
+        middle_cot = middle_cot + current_cot
+        out_cot = middle_cot.astype(bf16)
+        out_grad = jnp.einsum("rd,mrk->mdk", out_cot, context, preferred_element_type=f32)
+        context_cot = split_heads(
+            jnp.einsum("rd,mdk->mrk", out_cot, w_out, preferred_element_type=f32).astype(bf16)
+        )
+        raw = (
+            jnp.einsum("mqhe,mkhe->mhqk", queries_h, keys_h, preferred_element_type=f32)
+            * block_scale
+        )
+        attention = jnp.exp(raw - log_h)
+        value_cot = jnp.einsum(
+            "mhqk,mqhe->mkhe", attention.astype(bf16), context_cot, preferred_element_type=f32
+        )
+        prob_cot = jnp.einsum(
+            "mqhe,mkhe->mhqk", context_cot, values_h, preferred_element_type=f32
+        )
+        row_terms = jnp.sum(attention * prob_cot, axis=-1, keepdims=True)
+        score_cot = (attention * (prob_cot - row_terms) * block_scale).astype(bf16)
+        query_cot = jnp.einsum("mhqk,mkhe->mqhe", score_cot, keys_h, preferred_element_type=f32)
+        key_cot = jnp.einsum("mhqk,mqhe->mkhe", score_cot, queries_h, preferred_element_type=f32)
+        kv_cot = jnp.concatenate(
+            [
+                key_cot.reshape(4, 2 * own_rows, cols_m),
+                value_cot.reshape(4, 2 * own_rows, cols_m),
+            ],
+            axis=2,
+        )
+        theirs = sibling(kv_cot[:, own_rows:].astype(bf16), line)
+        kv_cot = (kv_cot[:, :own_rows] + theirs.astype(f32)).astype(bf16)
+        qkv_cot = jnp.concatenate(
+            [query_cot.astype(bf16).reshape(4, own_rows, cols_m), kv_cot], axis=2
+        )
+        qkv_grad = jnp.einsum("rd,mrk->mdk", normed, qkv_cot, preferred_element_type=f32)
+        normed_cot = jnp.einsum("mrk,mdk->rd", qkv_cot, w_qkv, preferred_element_type=f32)
+        input_cot, gain_parts[2 + 2 * l], bias_parts[2 + 2 * l] = norm_back(
+            current, gain_rows[2 + 2 * l], bias_rows[2 + 2 * l], normed_cot
+        )
+        current_cot = input_cot + middle_cot
+        layer_parts[l] = jnp.concatenate(
+            [g.astype(bf16) for g in (qkv_grad, out_grad, up_grad, down_grad)], axis=2
+        ).reshape(4, 2 * line, rows_d, 6 * cols_m)
+    down_in = current_cot.astype(bf16)
+    down_grad_t = transposed_times(down_in, cross_active)
+    active_cot = matmul(down_in, down_t)
+    hidden_cot = gelu_back(cross_hidden, active_cot).astype(bf16)
+    up_grad_t = transposed_times(hidden_cot, cross_hidden_in)
+    hidden_in_cot = matmul(hidden_cot, up_t)
+    after_cot, gain_parts[1], bias_parts[1] = norm_back(
+        after_cross, gain_rows[1], bias_rows[1], hidden_in_cot
+    )
+    after_cot = after_cot + current_cot
+    out_in = after_cot.astype(bf16)
+    cross_part = jnp.concatenate(
+        [
+            up_grad_t.astype(bf16).reshape(-1, own_cols, width),
+            down_grad_t.astype(bf16).reshape(-1, own_cols, width),
+        ],
+        axis=1,
+    ).reshape(2 * line, 4, 2 * own_cols, width)
+    reduced = reduce_all(
+        [layer_parts[l] for l in reversed(range(layers))] + [cross_part],
+        [True] * layers + [False],
+        line,
+    )
+
+    k_part = transposed_times(out_in, px_low).astype(bf16)
+    k_all = lax.psum(k_part, both_axes)
+    context_cot = matmul(out_in, out_t).astype(bf16)
+    cv = matmul(context_cot, value_t).astype(bf16)
+    delta = jnp.sum(cv.astype(f32) * px, axis=1)
+    rows_sent = jnp.pad(jnp.stack([log_total, delta], axis=0), ((0, 6), (0, 0)))
+    cv_all, rows_all = exchange([lanes(cv), rows_sent], "from_work", 4)
+    after_home = lax.ppermute(out_in, both_axes, back_moves)
+    cv_all = cv_all.reshape(items, 2 * half_rows, wide)[:, :, :channels]
+    log_all = rows_all[:, 0].reshape(items, 2 * half_rows)[:, :, None]
+    delta_all = rows_all[:, 1].reshape(items, 2 * half_rows)[:, :, None]
+    attention = jnp.exp(cross_scores() - log_all) * present.astype(f32)[:, None, :]
+    prob_cot = jnp.einsum("iqc,ipc->iqp", cv_all, pixel_in, preferred_element_type=f32)
+    score_cot = (attention * (prob_cot - delta_all)).astype(bf16)
+    dsx = jnp.einsum("iqp,ipc->iqc", score_cot, pixel_in, preferred_element_type=f32)
+    dsx = jnp.pad((dsx * scale).astype(bf16), ((0, 0), (0, 0), (0, pad)))
+    (dsx_parts,) = exchange([dsx.reshape(4, half_rows, wide)], "mp_split", 5)
+    dsx_own = jnp.sum(dsx_parts.astype(f32), axis=0)[:, :channels].astype(bf16)
+    pixel_in_cot = jnp.einsum(
+        "iqp,iqc->ipc", score_cot, qk_all, preferred_element_type=f32
+    ) + jnp.einsum("iqp,iqc->ipc", attention.astype(bf16), cv_all, preferred_element_type=f32)
+    pixel_cot, pixel_gain_part, pixel_bias_part = norm_back(
+        pixel_floats, pixel_gain_row, pixel_bias_row, pixel_in_cot
+    )
+    pixel_grad = pixel_cot.astype(bf16)
+    query_cot = times_transposed(dsx_own, key_t).astype(bf16)
+    query_in_cot = matmul(query_cot, query_t)
+    start_cot, gain_parts[0], bias_parts[0] = norm_back(
+        start_rows, gain_rows[0], bias_rows[0], query_in_cot
+    )
+    latent_grad = (start_cot + after_home.astype(f32)).astype(bf16)
+    g_part = transposed_times(query_in, dsx_own).astype(bf16)
+    g_all, small = lax.psum(
+        (
+            g_part,
+            (
+                jnp.stack(gain_parts, axis=0),
+                jnp.stack(bias_parts, axis=0),
+                pixel_gain_part,
+                pixel_bias_part,
+            ),
+        ),
+        both_axes,
+    )
+    cross_query_grad = matmul(g_all, cross_key)
+    cross_key_grad = transposed_times(g_all, cross_query)
+    at = (lax.axis_index("dp") * 4 + lax.axis_index("mp")) * own_cols
+    k_own = lax.dynamic_slice_in_dim(k_all, at, own_cols, 0)
+    cross_out_grad = lax.dot_general(
+        value_t, k_own, (((1,), (1,)), ((), ())), preferred_element_type=f32
+    )
+    out_own = lax.dynamic_slice_in_dim(out_t, at, own_cols, 1)
+    cross_value_grad = transposed_times(k_all, out_own)
+    gain_grad = lax.dynamic_slice_in_dim(small[0], at, own_cols, 1)
+    bias_grad = lax.dynamic_slice_in_dim(small[1], at, own_cols, 1)
+    layer_grads = [reduced[layers - 1 - l] for l in range(layers)]
+    qkv_out = jnp.stack(
+        [g[:, : 3 * cols_m].reshape(rows_d, 3, cols_m) for g in layer_grads], axis=0
+    )
+    out_out, up_out, down_out = [
+        jnp.stack([g[:, k * cols_m : (k + 1) * cols_m] for g in layer_grads], axis=0)
+        for k in (3, 4, 5)
+    ]
+    cross_sum = reduced[layers]
+    return (
+        latents_out,
+        latent_grad,
+        pixel_grad,
+        cross_query_grad,
+        cross_key_grad,
+        cross_value_grad,
+        cross_out_grad,
+        cross_sum[:own_cols].T,
+        cross_sum[own_cols:].T,
+        qkv_out,
+        out_out,
+        up_out,
+        down_out,
+        gain_grad,
+        bias_grad,
+        small[2],
+        small[3],
+    )
+
+
+def fits(mesh):
+    return mesh.shape["mp"] == 4 and mesh.shape["dp"] % 2 == 0
+
+
 def solution(mesh):
     return jax.shard_map(
-        shards,
+        fast_shards if fits(mesh) else shards,
         mesh=mesh,
         in_specs=(
             P(("dp", "mp"), None),

time: 2840 us -> 1050 us (0.37)
  waiting for transfers between devices: 1830 us -> 120 us
  blocking collectives: 430 us -> 45.2 us
  Pallas kernels: 0 us -> 366 us
  matrix products: 365 us -> 258 us
    reduce_scatter x22 -> x0, waiting for transfers between devices: 1060 us -> none  [the longest x5 172 us: sum_branch(): lax.psum_scatter(row_term(jnp.int32(0), own_rows * lax.axis_size('mp')).a...]
    all_gather x16 -> x0, waiting for transfers between devices: 387 us -> none  [the longest x5 175 us: gather_grads(): return lax.all_gather(payload, 'mp', axis=0, tiled=True)]
    unnamed x46 -> x1, waiting for transfers between devices: 384 us -> 0.02 us
    all_gather x12 -> x0, blocking collectives: 384 us -> none  [the longest x1 70.6 us: cross_params(): lax.all_gather(cross_key, ('dp', 'mp'), axis=1, tiled=True)]
    pallas_call x0 -> x6, Pallas kernels: none -> 366 us  [the longest x1 157 us: reduce_all(): pl.pallas_call(kernel, out_shape=tuple((jax.ShapeDtypeStruct(slab, jnp.fl...]
    psum x0 -> x1, waiting for transfers between devices: none -> 118 us  [fast_shards(): lax.psum((g_part, (jnp.stack(gain_parts, axis=0), jnp.stack(bias_parts, a...]
    dot_general x33 -> x43, matrix products: 298 us -> 224 us  [the longest x2 38.4 us: fast_shards(): jnp.einsum('mhqk,mqhe->mkhe', score_cot, queries_h, preferred_element_typ...]
    concatenate x0 -> x9, other arithmetic: none -> 43.8 us  [the longest x2 33.8 us: fast_shards(): jnp.concatenate([g.astype(bf16) for g in (qkv_grad, out_grad, up_grad, do...]
  transfers between devices with their start and end apart: 42 -> 9, of which waited for: 36 -> 2; matrix products, arithmetic and copies ran while one was open for 10% -> 25% of each run, Pallas kernels for 0% -> 33%
where the time goes in v1:
time: 1050 us; the launch traced here: 1030 us
  Pallas kernels  366 us (35%)
  matrix products  258 us (25%)
  waiting for transfers between devices  120 us (11%)
  local copies, waits for them, and re-layouts  107 us (10%)
  other arithmetic  103 us (10%)
  blocking collectives  45.2 us (4%)
  starting transfers between devices  20.3 us (2%)
  between operations  16.3 us (2%)
    pallas_call x1, Pallas kernels, reduce_all(): pl.pallas_call(kernel, out_shape=tuple((jax.ShapeDtypeStruct(slab, jnp.fl...  157 us
    pallas_call x1, Pallas kernels, gather_all(): pl.pallas_call(kernel, out_shape=shapes, in_specs=[ANY] * count, out_spec...  157 us
    psum x1, waiting for transfers between devices, fast_shards(): lax.psum((g_part, (jnp.stack(gain_parts, axis=0), jnp.stack(bias_parts, a...  118 us
    pallas_call x4, Pallas kernels, exchange(): pl.pallas_call(kernel, out_shape=shapes, in_specs=[ANY] * count, out_spec...  51.4 us
    psum x1, blocking collectives, fast_shards(): lax.psum((g_part, (jnp.stack(gain_parts, axis=0), jnp.stack(bias_parts, a...  45.2 us
    dot_general x2, matrix products, fast_shards(): jnp.einsum('mhqk,mqhe->mkhe', score_cot, queries_h, preferred_element_typ...  38.4 us
    dot_general x2, matrix products, fast_shards(): jnp.einsum('mhqk,mkhe->mqhe', score_cot, keys_h, preferred_element_type=f32)  37.2 us
    unnamed x230, local copies, waits for them, and re-layouts  34.2 us
  transfers between devices with their start and end apart: 9, of which 2 were waited for; matrix products, arithmetic and copies ran while one was open for 25% of the time, Pallas kernels for 33%

profile of v1, /device:TPU:0, one launch (start us, length us, event | category | flops | bytes accessed | tf_op | source)
XLA Modules:
  0.0 1034.4 jit_solution(9718220889408485553)
XLA Ops:
  7.2 5.5 collective-permute-start
  24.0 156.9 %weight_gather.1 = (bf16[8,4,32,1920]{3,2,1,0:T(8,128)(2,1)}, bf16[8,4,96,1024]{3,2,1,0:T(8,128)(2,1)}, bf16[4,8,128,1536]{3,2,1,0:T(8,128)(2,1)}, bf16[4,8,128,1536]{3,2,1,0:T(8,128)(2,1)}) custom-call(bf16[32,1920]{1,0:T(8,128)(2,1)} %fusion.303.refs_0_, bf16[96,1024]{1,0:T(8,128)(2,1)} %pad_maximum_fusion.19.refs_1_, ...), custom_call_target="tpu_custom_call" | custom-call | tf_op jit(solution)/shard_map/weight_gather/pallas_call | solution.py:811
  185.9 13.0 %exchange_mp.1 = bf16[4,256,384]{2,1,0:T(8,128)(2,1)} custom-call(bf16[256,384]{1,0:T(8,128)(2,1)} %pad.36.refs_0_), custom_call_target="tpu_custom_call" | custom-call | tf_op jit(solution)/shard_map/exchange_mp/pallas_call | solution.py:1143
  203.7 5.7 fusion.14
  209.6 9.0 select_reduce_fusion
  218.7 5.7 copy-done.7
  228.5 11.4 %fusion.185 = bf16[2,512,261]{1,2,0:T(8,128)(2,1)S(1)} fusion(f32[2,512,4096]{2,1,0:T(8,128)} %copy-done.7, f32[2,4096]{1,0:T(2,128)S(1)} %get-tuple-element.133, f32[2,512]{1,0:T(2,128)S(1)} %get-tuple-element.170, pred[2,4096]{1,0:T(4,128)(4,1)S(1)} %get-tuple-element.134, f32[261]{0:T(512)S(1)} %convert_element_type.309, ...), kind=kOutput, calls=%fused_computation.183 | convolution fusion | flops 2219299840 | bytes 21700648 | tf_op jit(solution)/shard_map/iqp,ipc->iqc/dot_general | solution.py:1268
  242.0 13.1 %exchange_to_work.1 = (bf16[4,256,384]{2,1,0:T(8,128)(2,1)}, f32[4,8,256]{2,1,0:T(8,128)}) custom-call(bf16[4,256,384]{2,1,0:T(8,128)(2,1)} %bitcast.291, f32[4,8,256]{2,1,0:T(8,128)} %pad.38.refs_1_), custom_call_target="tpu_custom_call" | custom-call | tf_op jit(solution)/shard_map/exchange_to_work/pallas_call | solution.py:1143
  258.8 6.0 fusion.370
  296.2 5.3 collective-permute-start.4
  329.9 19.1 %fusion.53 = f32[4,2,128,512]{3,2,1,0:T(8,128)} fusion(bf16[4,256,2,128]{1,3,2,0:T(8,128)(2,1)} %bitcast.309, f32[4,2,256,512]{3,2,1,0:T(8,128)} %fusion.386, f32[4,2,256,512]{3,2,1,0:T(8,128)} %copy-done.2, f32[4,2,256]{2,1,0:T(2,128)S(1)} %bitcast.388), kind=kOutput, calls=%fused_computation.69 | convolution fusion | flops 277875200 | bytes 11018240 | tf_op jit(solution)/shard_map/mhqk,mqhe->mkhe/dot_general | solution.py:1404
  354.7 18.5 %fusion.202 = bf16[4,2,128,256]{3,2,1,0:T(8,128)(2,1)} fusion(bf16[4,512,2,128]{1,3,2,0:T(8,128)(2,1)} %bitcast.286, f32[4,2,256,512]{3,2,1,0:T(8,128)} %fusion.386, f32[4,2,256,512]{3,2,1,0:T(8,128)} %copy-done.2, f32[4,2,256]{2,1,0:T(2,128)S(1)} %bitcast.389), kind=kOutput, calls=%fused_computation.193 | convolution fusion | flops 278137344 | bytes 9969664 | tf_op jit(solution)/shard_map/mhqk,mkhe->mqhe/dot_general | solution.py:1403
  409.8 19.3 %fusion.46 = f32[4,2,128,512]{3,2,1,0:T(8,128)} fusion(bf16[4,256,2,128]{1,3,2,0:T(8,128)(2,1)} %bitcast.307, f32[4,2,256,512]{3,2,1,0:T(8,128)} %fusion.387, f32[4,2,256,512]{3,2,1,0:T(8,128)} %copy-done, f32[4,2,256]{2,1,0:T(2,128)S(1)} %bitcast.383), kind=kOutput, calls=%fused_computation.66 | convolution fusion | flops 277875200 | bytes 11018240 | tf_op jit(solution)/shard_map/mhqk,mqhe->mkhe/dot_general | solution.py:1404
  436.4 18.0 %pad_maximum_fusion = bf16[4,1024,1536]{1,2,0:T(8,128)(2,1)} fusion(bf16[4,1024,256]{1,2,0:T(8,128)(2,1)} %convert_bitcast_fusion.5, bf16[4,1024,256]{1,2,0:T(8,128)(2,1)S(1)} %copy-done.23, bf16[4,1024,256]{1,2,0:T(8,128)(2,1)S(1)} %copy-done.22, bf16[4,1024,768]{1,2,0:T(8,128)(2,1)} %convert_bitcast_fusion.1), kind=kLoop, calls=%fused_computation.10 | loop fusion | flops 50331648 | bytes 25165824 | tf_op jit(solution)/shard_map/concatenate | solution.py:1423
  454.4 18.6 %fusion.205 = bf16[4,2,128,256]{3,2,1,0:T(8,128)(2,1)} fusion(bf16[4,512,2,128]{1,3,2,0:T(8,128)(2,1)} %bitcast.282, f32[4,2,256,512]{3,2,1,0:T(8,128)} %fusion.387, f32[4,2,256,512]{3,2,1,0:T(8,128)} %copy-done, f32[4,2,256]{2,1,0:T(2,128)S(1)} %bitcast.384), kind=kOutput, calls=%fused_computation.194 | convolution fusion | flops 278137344 | bytes 9969664 | tf_op jit(solution)/shard_map/mhqk,mkhe->mqhe/dot_general | solution.py:1403
  475.0 16.8 %copy.184 = bf16[4,1024,1536]{2,1,0:T(8,128)(2,1)} copy(bf16[4,1024,1536]{1,2,0:T(8,128)(2,1)} %pad_maximum_fusion) | data formatting | bytes 25165824 | tf_op jit(solution)/shard_map/concatenate | solution.py:1423
  502.7 5.2 multiply_reduce_fusion.8
  518.5 12.4 %exchange_from_work.1 = (bf16[4,256,384]{2,1,0:T(8,128)(2,1)}, f32[4,8,256]{2,1,0:T(8,128)}) custom-call(bf16[256,384]{1,0:T(8,128)(2,1)} %pad.39.refs_0_, f32[8,256]{1,0:T(8,128)} %select_maximum_fusion.refs_1_), custom_call_target="tpu_custom_call" | custom-call | tf_op jit(solution)/shard_map/exchange_from_work/pallas_call | solution.py:1143
  531.7 15.6 %multiply_convert_fusion = bf16[2,512,4096]{2,1,0:T(8,128)(2,1)} fusion(f32[2,512,4096]{2,1,0:T(8,128)} %copy-done.7, f32[2,512]{1,0:T(2,128)S(1)} %sub.217, f32[2,512]{1,0:T(2,128)S(1)} %sub.214, f32[2,4096]{1,0:T(2,128)S(1)} %get-tuple-element.133, pred[2,4096]{1,0:T(4,128)(4,1)S(1)} %get-tuple-element.134, bf16[2,512,384]{2,1,0:T(8,128)(2,1)} %bitcast.417, ...), kind=kOutput, calls=%fused_computation.2 | convolution fusion | flops 2227421184 | bytes 30345256 | tf_op jit(solution)/shard_map/iqc,ipc->iqp/dot_general | solution.py:1462
  547.4 10.4 %fusion.184 = bf16[2,512,261]{1,2,0:T(8,128)(2,1)} fusion(bf16[2,512,4096]{2,1,0:T(8,128)(2,1)} %multiply_convert_fusion, f32[261]{0:T(512)S(1)} %convert_element_type.309, f32[261]{0:T(512)S(1)} %convert_element_type.308, f32[2,4096]{1,0:T(2,128)S(1)} %fusion.309, f32[2,4096]{1,0:T(2,128)S(1)} %broadcast_multiply_fusion, ...), kind=kOutput, calls=%fused_computation.180 | convolution fusion | flops 2202789888 | bytes 13266984 | tf_op jit(solution)/shard_map/iqp,ipc->iqc/dot_general | solution.py:1464
  557.8 9.2 fusion.259
  581.1 12.9 %exchange_mp_split.1 = bf16[4,256,384]{2,1,0:T(8,128)(2,1)} custom-call(bf16[4,256,384]{2,1,0:T(8,128)(2,1)} %bitcast.292), custom_call_target="tpu_custom_call" | custom-call | tf_op jit(solution)/shard_map/exchange_mp_split/pallas_call | solution.py:1143
  600.6 5.3 collective-permute-start.7
  606.0 18.4 %fusion.361 = (f32[261]{0:T(512)S(1)}, f32[2,4096]{1,0:T(2,128)S(1)}, f32[2,4096,261]{1,2,0:T(8,128)}) fusion(f32[261]{0:T(512)S(1)} %convert_element_type.308, f32[2,4096]{1,0:T(2,128)S(1)} %broadcast_multiply_fusion, bf16[2,4096,261]{1,0,2:T(2,128)(2,1)} %param.19, f32[2,4096,261]{1,2,0:T(8,128)} %fusion.259, bf16[2,512,384]{2,1,0:T(8,128)(2,1)} %bitcast.418, ...), kind=kOutput, calls=%fused_computation.418 | convolution fusion | flops 2221162240 | bytes 39057448 | tf_op jit(solution)/shard_map/iqp,iqc->ipc/dot_general | solution.py:1470
  624.5 15.8 %pad_maximum_fusion.1 = bf16[4,1024,1536]{1,2,0:T(8,128)(2,1)} fusion(bf16[4,1024,256]{1,2,0:T(8,128)(2,1)} %convert_bitcast_fusion.2, bf16[4,1024,256]{1,2,0:T(8,128)(2,1)} %convert_bitcast_fusion.3, bf16[4,1024,256]{1,2,0:T(8,128)(2,1)} %convert_bitcast_fusion.4, bf16[4,1024,768]{1,2,0:T(8,128)(2,1)S(1)} %bitcast.275), kind=kLoop, calls=%fused_computation.11 | loop fusion | flops 50331648 | bytes 25165824 | tf_op jit(solution)/shard_map/concatenate | solution.py:1423
  640.3 16.8 %copy.186 = bf16[4,1024,1536]{2,1,0:T(8,128)(2,1)} copy(bf16[4,1024,1536]{1,2,0:T(8,128)(2,1)} %pad_maximum_fusion.1) | data formatting | bytes 25165824 | tf_op jit(solution)/shard_map/concatenate | solution.py:1423
  661.4 157.4 %grad_reduce.1 = (f32[128,1536]{1,0:T(8,128)}, f32[128,1536]{1,0:T(8,128)}, f32[64,1024]{1,0:T(8,128)}) custom-call(bf16[4,8,128,1536]{3,2,1,0:T(8,128)(2,1)} %bitcast.272, bf16[4,8,128,1536]{3,2,1,0:T(8,128)(2,1)} %bitcast.273, bf16[8,4,64,1024]{3,2,1,0:T(8,128)(2,1)} %pad_maximum_fusion.2.refs_2_), custom_call_target="tpu_custom_call" | custom-call | tf_op jit(solution)/shard_map/grad_reduce/pallas_call | solution.py:1054
  821.0 7.5 fusion.13
  828.6 7.9 add_convert_fusion
  839.3 45.2 %all-reduce.9 = (f32[6,1024]{1,0:T(8,128)S(1)}, f32[6,1024]{1,0:T(8,128)S(1)}, f32[261]{0:T(512)}, f32[261]{0:T(512)}) all-reduce(f32[6,1024]{1,0:T(8,128)S(1)} %stack.79, f32[6,1024]{1,0:T(8,128)S(1)} %stack.80, f32[261]{0:T(512)S(1)} %get-tuple-element.90, f32[261]{0:T(512)S(1)} %get-tuple-element.92), channel_id=1, replica_groups=mesh['dp'=8,'mp'=4] {'dp','mp'}, use_global_device_ids=true, to_apply=%region_49.50 | all-reduce | flops 12810 | bytes 102480 | tf_op jit(solution)/shard_map/psum | solution.py:1482
  888.5 8.8 copy.189
  900.3 117.7 %all-reduce.13.cloned.1.call-done = (bf16[1024,261]{0,1:T(8,128)(2,1)}, bf16[1024,261]{0,1:T(8,128)(2,1)}) async-done(((bf16[1024,261]{0,1:T(8,128)(2,1)}, bf16[1024,261]{0,1:T(8,128)(2,1)}), (bf16[1024,261]{0,1:T(8,128)(2,1)}, bf16[1024,261]{0,1:T(8,128)(2,1)})) %all-reduce.13.cloned.1.call-update) | async-done | bytes 1069072 | tf_op jit(solution)/shard_map/psum | solution.py:1482
  (420 shorter events, 209.4 us)
Async XLA Ops:
  7.2 174.9 %copy-start.24 = (bf16[256,1024]{1,0:T(8,128)(2,1)S(1)}, bf16[256,1024]{1,0:T(8,128)(2,1)}, u32[]{:S(2)}) copy-start(bf16[256,1024]{1,0:T(8,128)(2,1)} %param.18) | copy-start | bytes 1572868
  7.2 1010.8 %all-reduce.13.cloned.1.call-start = ((), (), s32[]{:S(2)}) async-start(), calls=%async_computation | async-start | bytes 2162688 | tf_op jit(solution)/shard_map/psum | solution.py:1482
  7.2 257.6 %collective-permute-start = (bf16[256,1024]{1,0:T(8,128)(2,1)}, bf16[256,1024]{1,0:T(8,128)(2,1)}, u32[]{:S(2)}, u32[]{:S(2)}) collective-permute-start(bf16[256,1024]{1,0:T(8,128)(2,1)} %param.18), channel_id=1, source_target_pairs={{0,0},{1,4},{2,1},{3,5},{4,2},{5,6},{6,3},{7,7},{8,8},{9,12},{10,9... | collective-permute-start | bytes 1572872 | tf_op jit(solution)/shard_map/ppermute | solution.py:1198
  182.0 16.9 %copy-start.72 = (f32[1,1024]{1,0:T(1,128)}, f32[1,1024]{1,0:T(1,128)S(1)}, u32[]{:S(2)}) copy-start(f32[1,1024]{1,0:T(1,128)S(1)} %get-tuple-element.169) | copy-start | bytes 12292
  182.0 16.9 %copy-start.86 = (f32[1,1024]{1,0:T(1,128)}, f32[1,1024]{1,0:T(1,128)S(1)}, u32[]{:S(2)}) copy-start(f32[1,1024]{1,0:T(1,128)S(1)} %get-tuple-element.168) | copy-start | bytes 12292
  182.1 86.4 %copy-start.78 = (f32[1,1024]{1,0:T(1,128)}, f32[1,1024]{1,0:T(1,128)S(1)}, u32[]{:S(2)}) copy-start(f32[1,1024]{1,0:T(1,128)S(1)} %get-tuple-element.166) | copy-start | bytes 12292
  182.1 90.5 %copy-start.76 = (f32[1,1024]{1,0:T(1,128)}, f32[1,1024]{1,0:T(1,128)S(1)}, u32[]{:S(2)}) copy-start(f32[1,1024]{1,0:T(1,128)S(1)} %get-tuple-element.164) | copy-start | bytes 12292
  182.1 16.9 %copy-start.74 = (f32[256]{0:T(256)}, f32[256]{0:T(256)S(1)}, u32[]{:S(2)}) copy-start(f32[256]{0:T(256)S(1)} %broadcast_multiply_fusion.6) | copy-start | bytes 3076
  182.4 21.3 %copy-start.82 = (f32[256]{0:T(256)}, f32[256]{0:T(256)S(1)}, u32[]{:S(2)}) copy-start(f32[256]{0:T(256)S(1)} %fusion.225) | copy-start | bytes 3076
  182.4 21.3 %copy-start.80 = (f32[256]{0:T(256)}, f32[256]{0:T(256)S(1)}, u32[]{:S(2)}) copy-start(f32[256]{0:T(256)S(1)} %fusion.316) | copy-start | bytes 3076
  203.7 24.8 %slice-start = ((s8[4276224]{0:T(1024)(128)(4,1)}), s8[81920]{0:T(1024)(128)(4,1)S(1)}, s32[]{:S(2)}) async-start(s8[4276224]{0:T(1024)(128)(4,1)} %bitcast.268), calls=%async_computation.1 | async-start | bytes 163840
  209.6 18.9 %slice-start.1 = ((s8[4276224]{0:T(1024)(128)(4,1)}), s8[4194304]{0:T(1024)(128)(4,1)S(1)}, s32[]{:S(2)}) async-start(s8[4276224]{0:T(1024)(128)(4,1)} %bitcast.268), calls=%async_computation.2 | async-start | bytes 8388608
  277.5 2.7 collective-permute-start.1
  291.5 17.7 %copy-start.10 = (f32[256,1024]{1,0:T(8,128)}, f32[256,1024]{1,0:T(8,128)S(1)}, u32[]{:S(2)}) copy-start(f32[256,1024]{1,0:T(8,128)S(1)} %get-tuple-element.181) | copy-start | bytes 3145732
  296.1 6.7 collective-permute-start.2
  296.2 20.0 %collective-permute-start.4 = (bf16[256,1024]{1,0:T(8,128)(2,1)}, bf16[256,1024]{1,0:T(8,128)(2,1)}, u32[]{:S(2)}, u32[]{:S(2)}) collective-permute-start(bf16[256,1024]{1,0:T(8,128)(2,1)} %param.35), channel_id=1, source_target_pairs={{0,0},{1,4},{2,1},{3,5},{4,2},{5,6},{6,3},{7,7},{8,8},{9,12},{10,9... | collective-permute-start | bytes 1572872 | tf_op jit(solution)/shard_map/ppermute | solution.py:1199
  306.1 19.6 %copy-start.2 = (f32[4,2,256,512]{3,2,1,0:T(8,128)}, f32[4,2,256,512]{3,2,1,0:T(8,128)S(1)}, u32[]{:S(2)}) copy-start(f32[4,2,256,512]{3,2,1,0:T(8,128)S(1)} %get-tuple-element.183) | copy-start | bytes 12582916
  354.7 30.9 %collective-permute-start.5 = (bf16[4,256,512]{2,1,0:T(8,128)(2,1)}, bf16[4,256,512]{2,1,0:T(8,128)(2,1)}, u32[]{:S(2)}, u32[]{:S(2)}) collective-permute-start(bf16[4,256,512]{2,1,0:T(8,128)(2,1)} %fusion.69), channel_id=1, source_target_pairs={{0,4},{1,5},{2,6},{3,7},{4,0},{5,1},{6,2},{7,3},{8,12},{9,13},{10,... | collective-permute-start | bytes 3145736 | tf_op jit(solution)/shard_map/ppermute | solution.py:1165
  375.3 9.5 collective-permute-start.3
  434.6 66.5 %collective-permute-start.6 = (bf16[4,256,512]{2,1,0:T(8,128)(2,1)}, bf16[4,256,512]{2,1,0:T(8,128)(2,1)}, u32[]{:S(2)}, u32[]{:S(2)}) collective-permute-start(bf16[4,256,512]{2,1,0:T(8,128)(2,1)} %fusion.68), channel_id=1, source_target_pairs={{0,4},{1,5},{2,6},{3,7},{4,0},{5,1},{6,2},{7,3},{8,12},{9,13},{10,... | collective-permute-start | bytes 3145736 | tf_op jit(solution)/shard_map/ppermute | solution.py:1165
  514.1 33.3 %slice-start.2 = ((s8[4276224]{0:T(1024)(128)(4,1)}), s8[81920]{0:T(1024)(128)(4,1)S(1)}, s32[]{:S(2)}) async-start(s8[4276224]{0:T(1024)(128)(4,1)} %bitcast.270), calls=%async_computation.3 | async-start | bytes 163840
  576.4 19.0 %copy-start.25 = (bf16[256,1024]{1,0:T(8,128)(2,1)S(1)}, bf16[256,1024]{1,0:T(8,128)(2,1)}, u32[]{:S(2)}) copy-start(bf16[256,1024]{1,0:T(8,128)(2,1)} %param.18) | copy-start | bytes 1572868
  576.4 19.0 %copy-start.73 = (f32[1,1024]{1,0:T(1,128)S(1)}, f32[1,1024]{1,0:T(1,128)}, u32[]{:S(2)}) copy-start(f32[1,1024]{1,0:T(1,128)} %copy-done.72) | copy-start | bytes 12292
  576.4 19.0 %copy-start.75 = (f32[256]{0:T(256)S(1)}, f32[256]{0:T(256)}, u32[]{:S(2)}) copy-start(f32[256]{0:T(256)} %copy-done.74) | copy-start | bytes 3076
  600.6 297.4 %collective-permute-start.7 = (bf16[256,1024]{1,0:T(8,128)(2,1)}, bf16[256,1024]{1,0:T(8,128)(2,1)}, u32[]{:S(2)}, u32[]{:S(2)}) collective-permute-start(bf16[256,1024]{1,0:T(8,128)(2,1)} %add_convert_fusion.2), channel_id=1, source_target_pairs={{0,0},{4,1},{1,2},{5,3},{2,4},{6,5},{3,6},{7,7},{8,8},{12,9},{9,10... | collective-permute-start | bytes 1572872 | tf_op jit(solution)/shard_map/ppermute | solution.py:1457
  606.0 18.5 %slice-start.4 = ((s8[6291456]{0:T(1024)(128)(4,1)}), s8[4194304]{0:T(1024)(128)(4,1)S(1)}, s32[]{:S(2)}) async-start(s8[6291456]{0:T(1024)(128)(4,1)} %bitcast.274), calls=%async_computation.5 | async-start | bytes 8388608
  606.0 18.4 %copy-start.68 = (f32[2,4096]{1,0:T(2,128)S(1)}, f32[2,4096]{1,0:T(2,128)}, u32[]{:S(2)}) copy-start(f32[2,4096]{1,0:T(2,128)} %copy-done.67) | copy-start | bytes 98308
  606.0 18.5 %slice-start.5 = ((s8[6291456]{0:T(1024)(128)(4,1)}), s8[2097152]{0:T(1024)(128)(4,1)S(1)}, s32[]{:S(2)}) async-start(s8[6291456]{0:T(1024)(128)(4,1)} %bitcast.274), calls=%async_computation.6 | async-start | bytes 4194304
  836.4 49.8 %copy-start.57 = (f32[128,1536]{1,0:T(8,128)S(1)}, f32[128,1536]{1,0:T(8,128)}, u32[]{:S(2)}) copy-start(f32[128,1536]{1,0:T(8,128)} %get-tuple-element.38) | copy-start | bytes 2359300
  897.3 125.2 %copy-start.71 = (bf16[261,32]{0,1:T(8,128)(2,1)S(1)}, bf16[261,32]{0,1:T(8,128)(2,1)}, u32[]{:S(2)}) copy-start(bf16[261,32]{0,1:T(8,128)(2,1)} %param.22) | copy-start | bytes 50116
  897.3 127.1 %copy-start.70 = (bf16[1024,32]{0,1:T(8,128)(2,1)S(1)}, bf16[1024,32]{0,1:T(8,128)(2,1)}, u32[]{:S(2)}) copy-start(bf16[1024,32]{0,1:T(8,128)(2,1)} %param.21) | copy-start | bytes 196612
  897.3 129.1 %copy-start.64 = (bf16[256,1024]{1,0:T(8,128)(2,1)S(1)}, bf16[256,1024]{1,0:T(8,128)(2,1)}, u32[]{:S(2)}) copy-start(bf16[256,1024]{1,0:T(8,128)(2,1)} %copy-done.63) | copy-start | bytes 1572868
  (87 other events, 472.9 us)
Sparse Core Ops, SparseCore 0:
  886.7 131.2 all-reduce.12
